TPU v7x, 512 devices: a whole 4x4x16 slice. The times are simulated.
512 devices in a mesh: tower: 2 (over core), seq: 64 (over y, x, z_hi), head: 4 (over z_lo).
Axes of the slice: x: 4, y: 4, z: 16 (z_hi: 4, z_lo: 4; z = z_hi * 4 + z_lo), core: 2. Of those that a mesh axis runs over, the one named last changes fastest.
Arguments:
- queries: bfloat16 [2, 4096, 3072], P('tower', ('seq', 'head')), may hold values from -100 to 100
- key_rows: bfloat16 [2, 4096, 3072], P('tower', ('seq', 'head')), may hold values from -4 to 4
- value_rows: bfloat16 [2, 4096, 3072], P('tower', ('seq', 'head')), may hold values from -6 to 6
- hidden: bfloat16 [2, 4096, 3072], P('tower', 'seq', 'head'), may hold values from -6 to 6
- gate_table: bfloat16 [2, 1000, 3072], P('tower', None, 'head'), may hold values from -8 to 8
- lengths: int32 [2, 1, 3], replicated, may hold values from 1 to 2048, 4096 in all within a row
- step_ids: int32 [1, 3], replicated, may hold values from 0 to 999
Outputs:
- mixed: bfloat16 [2, 4096, 3072], P('tower', 'seq', 'head')
Inputs may be any that keep to these rules, and one draw needn't show every extreme that they name: Each row holds the lengths of the 3 samples of one pack in order and sums to 4096; its largest entry is 2048; sample k of a pack is the same clip in both towers.
All inputs are finite; a program needn't handle non-finite values.
Results may differ from a plain program's by a relative error of at most 0.0034.
Values may be sent and summed in bfloat16 or wider, within the bound.
No kernel may reach another device: no remote copies, remote signals or barrier semaphores. Data moves between devices by JAX's collectives and lax.ppermute only.
A program may use at most 128 MiB of HBM per device.

v0:
```python
import jax
import jax.numpy as jnp
from jax import lax
from jax.sharding import PartitionSpec as P

HEAD_DIM = 128


def partner(block, axis, stride):
    count = lax.axis_size(axis)
    route = []
    for low in range(count):
        high = low | 1 << stride
        if high != low and high < count:
            route += [(low, high), (high, low)]
    return lax.ppermute(block, axis, route)


def sample_ids(positions, pack_lengths):
    bounds = jnp.cumsum(pack_lengths)[:-1]
    return jnp.sum((positions[:, None] >= bounds[None, :]).astype(jnp.int32), axis=1)


def pick_entry(small_table, wanted):
    matches = jnp.arange(small_table.shape[0], dtype=jnp.int32) == wanted
    matches = matches.reshape((-1,) + (1,) * (small_table.ndim - 1))
    return jnp.sum(jnp.where(matches, small_table, jnp.zeros_like(small_table)), axis=0)


def attend(query_rows, key_block, value_block, query_ids, key_ids):
    shard_rows = query_rows.shape[0]
    head_count = query_rows.shape[1] // HEAD_DIM
    block_size = min(512, key_block.shape[0])
    block_count = key_block.shape[0] // block_size
    score_scale = HEAD_DIM ** (-0.5)

    def compute(operands):
        query_part, key_part, ids_part = operands
        scores = (
            jnp.einsum("qd,kd->qk", query_part, key_part, preferred_element_type=jnp.float32)
            * score_scale
        )
        return jnp.where(query_ids[:, None] == ids_part[None, :], scores, -1e30)

    def one_head(head_index):
        first_col = head_index * HEAD_DIM
        query_head = lax.dynamic_slice_in_dim(query_rows, first_col, HEAD_DIM, 1)
        key_head = lax.dynamic_slice_in_dim(key_block, first_col, HEAD_DIM, 1)
        value_head = lax.dynamic_slice_in_dim(value_block, first_col, HEAD_DIM, 1)
        pieces = []
        for block_index in range(block_count):
            first_row = block_index * block_size
            operands = (
                query_head,
                key_head[first_row : first_row + block_size],
                key_ids[first_row : first_row + block_size],
            )
            pieces.append(compute(operands))
        scores = jnp.concatenate(pieces, axis=1)
        row_max = jnp.max(scores, axis=1, keepdims=True)
        expterm = jnp.exp(scores - row_max)
        weights = (expterm / jnp.sum(expterm, axis=1, keepdims=True)).astype(jnp.bfloat16)
        return jnp.dot(weights, value_head, preferred_element_type=jnp.float32)

    per_head = lax.map(one_head, jnp.arange(head_count, dtype=jnp.int32))
    return jnp.moveaxis(per_head, 0, 1).reshape(shard_rows, head_count * HEAD_DIM)


def shards(queries, key_rows, value_rows, hidden, gate_table, lengths, step_ids):
    tower_index = lax.axis_index("tower")
    seq_index = lax.axis_index("seq")
    span_count = lax.axis_size("seq")
    pack_index = seq_index // span_count
    pack_slot = seq_index % span_count
    grouped = lax.all_to_all(
        jnp.concatenate([queries, key_rows, value_rows], axis=0),
        "head",
        split_axis=2,
        concat_axis=1,
        tiled=True,
    )
    query_rows = grouped[0]
    far_pair = partner(grouped[1:], "tower", 0)
    shard_rows = far_pair.shape[1]
    pack_pair = lax.all_gather(far_pair, "seq", axis=1, tiled=True)
    own_lengths = pick_entry(pick_entry(lengths, tower_index), pack_index)
    far_lengths = pick_entry(pick_entry(lengths, 1 - tower_index), pack_index)
    positions = pack_slot * shard_rows + jnp.arange(shard_rows, dtype=jnp.int32)
    query_ids = sample_ids(positions, own_lengths)
    key_ids = sample_ids(jnp.arange(span_count * shard_rows, dtype=jnp.int32), far_lengths)
    attended = attend(query_rows, pack_pair[0], pack_pair[1], query_ids, key_ids)
    pack_steps = pick_entry(step_ids, pack_index)
    sample_range = jnp.arange(pack_steps.shape[0], dtype=jnp.int32)
    row_steps = jnp.sum(
        jnp.where(query_ids[:, None] == sample_range[None, :], pack_steps[None, :], 0), axis=1
    )
    selector = (
        row_steps[:, None] == jnp.arange(gate_table.shape[1], dtype=jnp.int32)[None, :]
    ).astype(jnp.bfloat16)
    gate_rows = jnp.dot(selector, gate_table[0], preferred_element_type=jnp.float32)
    combined = (hidden[0].astype(jnp.float32) + gate_rows * attended).astype(jnp.bfloat16)
    return combined[None]


def solution(mesh):
    return jax.shard_map(
        shards,
        mesh=mesh,
        in_specs=(
            P("tower", ("seq", "head"), None),
            P("tower", ("seq", "head"), None),
            P("tower", ("seq", "head"), None),
            P("tower", "seq", "head"),
            P("tower", None, "head"),
            P(),
            P(),
        ),
        out_specs=P("tower", "seq", "head"),
        check_vma=False,
    )
```

profile of v0, /device:TPU:1, one launch (start us, length us, event | category | flops | bytes accessed | tf_op | source)
XLA Modules:
  0.0 390.9 jit_solution(18125922978846744471)
XLA Ops:
  7.7 3.6 copy.22
  11.3 4.4 %reshape.118 = bf16[4,2,18432]{2,1,0:T(2,128)(2,1)S(1)} reshape(bf16[3072,3,16]{2,1,0:T(4,128)(2,1)} %bitcast.54) | data formatting | bytes 589824
  15.7 12.9 %all_to_all.15 = bf16[4,2,18432]{2,1,0:T(2,128)(2,1)S(1)} all-to-all(bf16[4,2,18432]{2,1,0:T(2,128)(2,1)S(1)} %reshape.118), channel_id=1, replica_groups=mesh['tower'=2,'seq'=64,'head'=4] {'head'}, dimensions={0} | all-to-all | bytes 589824 | tf_op jit(solution)/shard_map/all_to_all | solution.py:75
  28.5 4.1 %reshape.119 = bf16[3072,3,16]{2,1,0:T(4,128)(2,1)} reshape(bf16[4,2,18432]{2,1,0:T(2,128)(2,1)S(1)} %all_to_all.15) | data formatting | bytes 589824
  32.6 3.6 slice.80
  37.1 6.0 %collective-permute-start = (bf16[2,64,768]{2,1,0:T(8,128)(2,1)S(1)}, bf16[2,64,768]{2,1,0:T(8,128)(2,1)S(1)}, u32[]{:S(2)}, u32[]{:S(2)}) collective-permute-start(bf16[2,64,768]{2,1,0:T(8,128)(2,1)S(1)} %bitcast.56), channel_id=1, source_target_pairs={{0,256},{256,0},{1,257},{257,1},{2,258},{258,2},{3,259},{259,3},{4... | collective-permute-start | bytes 589832 | tf_op jit(solution)/shard_map/ppermute | solution.py:16
  45.8 3.0 slice.79
  49.5 245.5 %all-gather.2.cloned.1.call-done = bf16[2,4096,768]{2,1,0:T(8,128)(2,1)} async-done(((bf16[2,64,768]{2,1,0:T(8,128)(2,1)}), bf16[2,4096,768]{2,1,0:T(8,128)(2,1)}) %all-gather.2.cloned.1.call-update) | async-done | bytes 12582928 | tf_op jit(solution)/shard_map/all_gather | solution.py:85
  295.0 10.3 %slice_bitcast_fusion = (bf16[4096,768]{1,0:T(8,128)(2,1)}, bf16[4096,768]{1,0:T(8,128)(2,1)}) fusion(bf16[2,4096,768]{2,1,0:T(8,128)(2,1)} %all-gather.2.cloned.1.call-done), kind=kLoop, calls=%fused_computation.44 | loop fusion | bytes 25165824 | tf_op jit(solution)/shard_map/squeeze | solution.py:91
  305.4 77.5 %while.10 = (s32[]{:T(128)}, f32[6,64,128]{2,1,0:T(8,128)S(1)}, s32[64]{0:T(128)S(1)}, s32[4096]{0:T(1024)S(1)}, s32[6]{0:T(128)S(1)}, /*index=5*/bf16[64,768]{1...) while((s32[]{:T(128)}, f32[6,64,128]{2,1,0:T(8,128)S(1)}, ...), condition=%wide.region_17.18_spmd, body=%wide.region_7.17_spmd.sunk | while | flops 136576896 | bytes 5480011 | solution.py:65
  309.1 1.2 fusion.71
  311.5 1.2 fusion.73
  313.9 1.2 fusion.75
  315.1 1.2 fusion.76
  316.7 1.6 fusion.78
  320.9 1.2 fusion.70
  322.1 1.2 fusion.71
  329.6 1.6 fusion.78
  333.8 1.2 fusion.70
  337.4 1.2 fusion.73
  342.5 1.6 fusion.78
  346.7 1.2 fusion.70
  350.3 1.2 fusion.73
  351.5 1.2 fusion.74
  355.4 1.6 fusion.78
  358.5 1.2 fusion.69
  359.7 1.2 fusion.70
  360.9 1.2 fusion.71
  362.0 1.2 fusion.72
  368.4 1.6 fusion.78
  372.6 1.2 fusion.70
  381.3 1.6 fusion.78
  (88 shorter events, 50.6 us)
Async XLA Ops:
  6.5 376.4 %copy-start = (bf16[1,1000,768]{2,1,0:T(8,128)(2,1)S(1)}, bf16[1,1000,768]{2,1,0:T(8,128)(2,1)}, u32[]{:S(2)}) copy-start(bf16[1,1000,768]{2,1,0:T(8,128)(2,1)} %param.13) | copy-start | bytes 4608004
  6.5 288.5 %all-gather.2.cloned.1.call-start = ((), (), s32[]{:S(2)}) async-start(), calls=%async_computation.1 | async-start | bytes 12779520 | tf_op jit(solution)/shard_map/all_gather | solution.py:85
  11.2 33.8 %copy-start.3 = (s32[2,1,3]{2,1,0:T(1,128)S(1)}, s32[2,1,3]{2,1,0:T(1,128)}, u32[]{:S(2)}) copy-start(s32[2,1,3]{2,1,0:T(1,128)} %param.14) | copy-start | bytes 76
  11.3 34.3 %copy-start.4 = (s32[1,3]{1,0:T(1,128)S(1)}, s32[1,3]{1,0:T(1,128)}, u32[]{:S(2)}) copy-start(s32[1,3]{1,0:T(1,128)} %param.15) | copy-start | bytes 40
  37.1 7.1 %collective-permute-start = (bf16[2,64,768]{2,1,0:T(8,128)(2,1)S(1)}, bf16[2,64,768]{2,1,0:T(8,128)(2,1)S(1)}, u32[]{:S(2)}, u32[]{:S(2)}) collective-permute-start(bf16[2,64,768]{2,1,0:T(8,128)(2,1)S(1)} %bitcast.56), channel_id=1, source_target_pairs={{0,256},{256,0},{1,257},{257,1},{2,258},{258,2},{3,259},{259,3},{4... | collective-permute-start | bytes 589832 | tf_op jit(solution)/shard_map/ppermute | solution.py:16
  44.2 0.7 copy-start.1
  305.4 77.6 %copy-start.2 = (bf16[1,64,768]{2,1,0:T(8,128)(2,1)S(1)}, bf16[1,64,768]{2,1,0:T(8,128)(2,1)}, u32[]{:S(2)}) copy-start(bf16[1,64,768]{2,1,0:T(8,128)(2,1)} %param.12) | copy-start | bytes 294916
Sparse Core Ops, SparseCore 0:
  45.1 249.9 all-gather.1
where the time goes:
time: 392 us; the launch traced here: 391 us
  waiting for transfers between devices  247 us (63%)
  matrix products  67.9 us (17%)
  local copies, waits for them, and re-layouts  35.3 us (9%)
  between operations  13.5 us (3%)
  blocking collectives  12.9 us (3%)
  starting transfers between devices  6.05 us (2%)
  loops' own time  4.65 us (1%)
  other arithmetic  3.92 us (1%)
    all_gather x1, waiting for transfers between devices, shards(): pack_pair = lax.all_gather(far_pair, 'seq', axis=1, tiled=True)  246 us
    dot_general x48, matrix products, compute(): jnp.einsum('qd,kd->qk', query_part, key_part, preferred_element_type=jnp....  57.2 us
    all_to_all x1, blocking collectives, shards(): lax.all_to_all(jnp.concatenate([queries, key_rows, value_rows], axis=0),...  12.9 us
    squeeze x1, local copies, waits for them, and re-layouts, shards(): pack_pair[1]  10.3 us
    dot_general x6, matrix products, one_head(): return jnp.dot(weights, value_head, preferred_element_type=jnp.float32)  9.67 us
    unnamed x12, local copies, waits for them, and re-layouts  9.15 us
  transfers between devices with their start and end apart: 2, of which 2 were waited for; matrix products, arithmetic and copies ran while one was open for 1% of the time, Pallas kernels for 0%

commit v1 on v0

v1 whole, which is shorter than its diff:
```python
import functools

import jax
import jax.numpy as jnp
from jax import lax
from jax.experimental import pallas as pl
from jax.experimental.pallas import tpu as pltpu
from jax.sharding import Mesh, PartitionSpec as P

HEAD_DIM = 128
SCALE = HEAD_DIM**-0.5 * 1.4426950408889634
MASKED = -(2.0**100)
COLUMNS = ("y", "x")
STATS = 128


def sample_of(positions, bound_a, bound_b):
    return (positions >= bound_a).astype(jnp.int32) + (positions >= bound_b).astype(jnp.int32)


def pack_kernel(q_ref, k_ref, v_ref, kv_ref, qs_ref):
    groups, rows, width = qs_ref.shape
    for g in range(groups):
        cols = slice(g * width, (g + 1) * width)
        qs_ref[g] = q_ref[0, :, cols]
        kv_ref[g, :rows] = k_ref[0, :, cols]
        kv_ref[g, rows:] = v_ref[0, :, cols]


def attend_kernel(info_ref, q_ref, *refs):
    kv_refs, out_ref = refs[:-1], refs[-1]
    columns, rows, width = q_ref.shape
    heads = width // HEAD_DIM
    chunks = len(kv_refs)
    sources, pair_rows, _ = kv_refs[0].shape
    part = pair_rows // 2
    per_chunk = sources * part
    keys = chunks * per_chunk
    own_a, own_b, far_a, far_b = (info_ref[i] for i in range(4))
    first_key, zhi = info_ref[4], info_ref[5]

    lane = lax.broadcasted_iota(jnp.int32, (1, keys), 1)
    key_at = first_key + lax.rem(lane // per_chunk + zhi, chunks) * per_chunk + lane % per_chunk
    key_ids = sample_of(key_at, far_a, far_b)
    stat_lane = lax.broadcasted_iota(jnp.int32, (1, STATS), 1)
    block = 4
    tile = block * rows

    def step(t, _):
        r = lax.broadcasted_iota(jnp.int32, (tile, 1), 0)
        query_at = ((t * block + r // rows) * chunks + zhi) * rows + r % rows
        allowed = sample_of(query_at, own_a, own_b) == key_ids
        stats = jnp.zeros((tile, STATS), jnp.float32)
        for h in range(heads):
            cols = slice(h * HEAD_DIM, (h + 1) * HEAD_DIM)
            q = q_ref[pl.ds(t * block, block), :, cols].reshape(tile, HEAD_DIM)
            k = jnp.concatenate(
                [ref[s, :part, cols] for ref in kv_refs for s in range(sources)], axis=0
            )
            v = jnp.concatenate(
                [ref[s, part:, cols] for ref in kv_refs for s in range(sources)], axis=0
            )
            v = jnp.concatenate([v, jnp.ones((keys, HEAD_DIM), v.dtype)], axis=1)
            s = lax.dot_general(q, k, (((1,), (1,)), ((), ())), preferred_element_type=jnp.float32)
            s = jnp.where(allowed, s * SCALE, MASKED)
            top = jnp.max(s, axis=1, keepdims=True).astype(jnp.bfloat16).astype(jnp.float32)
            p = jnp.exp2(s - top).astype(jnp.bfloat16)
            o = jnp.dot(p, v, preferred_element_type=jnp.float32)
            out_ref[pl.ds(t * block, block), :, cols] = (
                o[:, :HEAD_DIM].astype(jnp.bfloat16).reshape(block, rows, HEAD_DIM)
            )
            total = o[:, HEAD_DIM:]
            high = total.astype(jnp.bfloat16).astype(jnp.float32)
            stats = jnp.where(stat_lane == h, top, stats)
            stats = jnp.where(stat_lane == 32 + h, high, stats)
            stats = jnp.where(stat_lane == 64 + h, total - high, stats)
        out_ref[pl.ds(t * block, block), :, width:] = stats.astype(jnp.bfloat16).reshape(
            block, rows, STATS
        )
        return 0

    lax.fori_loop(0, columns // block, step, 0)


def merge_kernel(info_ref, parts_ref, hidden_ref, gates_ref, out_ref):
    columns, rows, full = parts_ref.shape
    width = full - STATS
    heads = width // HEAD_DIM
    own_a, own_b, first_row = info_ref[0], info_ref[1], info_ref[6]
    stats = [parts_ref[j, :, width:].astype(jnp.float32) for j in range(columns)]
    top = functools.reduce(jnp.maximum, stats)
    scales, total = [], jnp.zeros_like(top)
    for st in stats:
        scale = jnp.exp2(jnp.minimum(st - top, 0.0))
        sums = pltpu.roll(st, STATS - 32, 1) + pltpu.roll(st, STATS - 64, 1)
        scales.append(scale)
        total = total + scale * sums
    inverse = 1.0 / total
    scales = [scale * inverse for scale in scales]
    at = first_row + lax.broadcasted_iota(jnp.int32, (rows, 1), 0)
    ids = sample_of(at, own_a, own_b)
    for h in range(heads):
        cols = slice(h * HEAD_DIM, (h + 1) * HEAD_DIM)
        o = jnp.zeros((rows, HEAD_DIM), jnp.float32)
        for j in range(columns):
            o = o + scales[j][:, h : h + 1] * parts_ref[j, :, cols].astype(jnp.float32)
        gate = jnp.where(
            ids == 0,
            gates_ref[0:1, cols],
            jnp.where(ids == 1, gates_ref[1:2, cols], gates_ref[2:3, cols]),
        )
        out_ref[0, :, cols] = (hidden_ref[0, :, cols].astype(jnp.float32) + gate * o).astype(
            jnp.bfloat16
        )


def vmem(n):
    return [pl.BlockSpec(memory_space=pltpu.VMEM)] * n


SMEM = pl.BlockSpec(memory_space=pltpu.SMEM)
PARAMS = pltpu.CompilerParams(vmem_limit_bytes=40 * 1024 * 1024)


def shards(queries, key_rows, value_rows, hidden, gate_table, lengths, step_ids):
    groups = lax.axis_size("head")
    columns = lax.axis_size(COLUMNS)
    chunks = lax.axis_size("zhi")
    tower, zhi, column = lax.axis_index("tower"), lax.axis_index("zhi"), lax.axis_index(COLUMNS)
    rows, width = queries.shape[1], queries.shape[2] // groups
    own_rows = rows * groups

    kv, qs = pl.pallas_call(
        pack_kernel,
        out_shape=(
            jax.ShapeDtypeStruct((groups, 2 * rows, width), jnp.bfloat16),
            jax.ShapeDtypeStruct((groups, rows, width), jnp.bfloat16),
        ),
        in_specs=vmem(3),
        out_specs=tuple(vmem(2)),
        name="pack",
    )(queries, key_rows, value_rows)

    kv = lax.all_to_all(kv, "head", 0, 0, tiled=True)
    far = []
    for shift in range(chunks):
        route = [
            (t * chunks + (z + shift) % chunks, (1 - t) * chunks + z)
            for t in range(2)
            for z in range(chunks)
        ]
        far.append(lax.ppermute(kv, ("tower", "zhi"), route))

    qs = lax.all_to_all(qs, "head", 0, 0, tiled=True).reshape(own_rows, width)
    qs = jnp.broadcast_to(qs[None], (columns, own_rows, width))
    qs = lax.all_to_all(qs, COLUMNS, 0, 0, tiled=True)

    flat = lengths[:, 0, :]
    own = lax.dynamic_index_in_dim(flat, tower, 0, False)
    other = lax.dynamic_index_in_dim(flat, 1 - tower, 0, False)
    info = jnp.stack(
        [
            own[0],
            own[0] + own[1],
            other[0],
            other[0] + other[1],
            column * chunks * own_rows,
            zhi,
            (column * chunks + zhi) * own_rows,
            jnp.int32(0),
        ]
    ).astype(jnp.int32)
    wanted = jnp.zeros((8,), jnp.int32).at[:3].set(step_ids[0])
    selector = wanted[:, None] == jnp.arange(gate_table.shape[1], dtype=jnp.int32)[None, :]
    gates = jnp.dot(
        selector.astype(jnp.bfloat16), gate_table[0], preferred_element_type=jnp.float32
    )

    parts = pl.pallas_call(
        attend_kernel,
        out_shape=jax.ShapeDtypeStruct((columns, own_rows, width + STATS), jnp.bfloat16),
        in_specs=[SMEM] + vmem(1 + chunks),
        out_specs=vmem(1)[0],
        compiler_params=PARAMS,
        name="attend",
    )(info, qs, *far)
    parts = lax.all_to_all(parts, COLUMNS, 0, 0, tiled=True)
    return pl.pallas_call(
        merge_kernel,
        out_shape=jax.ShapeDtypeStruct(hidden.shape, jnp.bfloat16),
        in_specs=[SMEM] + vmem(3),
        out_specs=vmem(1)[0],
        compiler_params=PARAMS,
        name="merge",
    )(info, parts, hidden, gates)


def solution(mesh):
    towers, seq, head = mesh.devices.shape
    fine = Mesh(
        mesh.devices.reshape(towers, 4, 4, seq // 16, head), ("tower", "y", "x", "zhi", "head")
    )
    rows = P("tower", ("y", "x", "zhi", "head"), None)
    block = P("tower", ("y", "x", "zhi"), "head")
    return jax.shard_map(
        shards,
        mesh=fine,
        in_specs=(rows, rows, rows, block, P("tower", None, "head"), P(), P()),
        out_specs=block,
        check_vma=False,
    )
```

time: 392 us -> 128 us (0.33)
  the two profiles are of different devices: /device:TPU:1 before, /device:TPU:96 now
where the time goes in v1:
time: 128 us; the launch traced here: 127 us
  waiting for transfers between devices  52.6 us (41%)
  starting transfers between devices  36.3 us (28%)
  blocking collectives  22 us (17%)
  Pallas kernels  8.66 us (7%)
  local copies, waits for them, and re-layouts  4.61 us (4%)
  between operations  2.72 us (2%)
    all_to_all x1, waiting for transfers between devices, shards(): parts = lax.all_to_all(parts, COLUMNS, 0, 0, tiled=True)  28.1 us
    ppermute x4, starting transfers between devices, shards(): far.append(lax.ppermute(kv, ('tower', 'zhi'), route))  24.6 us
    ppermute x4, waiting for transfers between devices, shards(): far.append(lax.ppermute(kv, ('tower', 'zhi'), route))  24.5 us
    all_to_all x1, blocking collectives, shards(): kv = lax.all_to_all(kv, 'head', 0, 0, tiled=True)  11 us
    all_to_all x1, blocking collectives, shards(): qs = lax.all_to_all(qs, 'head', 0, 0, tiled=True).reshape(own_rows, width)  10.9 us
    all_to_all x1, starting transfers between devices, shards(): parts = lax.all_to_all(parts, COLUMNS, 0, 0, tiled=True)  7.33 us
    pallas_call x1, Pallas kernels, shards(): pl.pallas_call(attend_kernel, out_shape=jax.ShapeDtypeStruct((columns, ow...  4.46 us
    all_to_all x1, starting transfers between devices, shards(): qs = lax.all_to_all(qs, COLUMNS, 0, 0, tiled=True)  4.41 us
  transfers between devices with their start and end apart: 6, of which 4 were waited for; matrix products, arithmetic and copies ran while one was open for 2% of the time, Pallas kernels for 0%

profile of v1, /device:TPU:96, one launch (start us, length us, event | category | flops | bytes accessed | tf_op | source)
XLA Modules:
  0.0 127.2 jit_solution(18415339122961123937)
XLA Ops:
  0.0 0.0 copy-start
  0.0 1.8 %pack.1 = (bf16[4,32,768]{2,1,0:T(8,128)(2,1)}, bf16[4,16,768]{2,1,0:T(8,128)(2,1)}) custom-call(bf16[1,16,3072]{2,1,0:T(8,128)(2,1)} %q_ref.1, bf16[1,16,3072]{2,1,0:T(8,128)(2,1)} %k_ref.1, bf16[1,16,3072]{2,1,0:T(8,128)(2,1)} %v_ref.1), custom_call_target="tpu_custom_call" | custom-call | tf_op jit(solution)/shard_map/pack/pallas_call | solution.py:133
  1.8 10.9 %all_to_all.20 = bf16[4,16,768]{2,1,0:T(8,128)(2,1)S(1)} all-to-all(bf16[4,16,768]{2,1,0:T(8,128)(2,1)} %get-tuple-element.19), channel_id=1, replica_groups=mesh['tower'=2,'y'=4,'x'=4,'zhi'=4,'head'=4] {'head'}, dimensions={0} | all-to-all | bytes 196608 | tf_op jit(solution)/shard_map/all_to_all | solution.py:154
  12.8 11.0 %all_to_all.21 = bf16[4,32,768]{2,1,0:T(8,128)(2,1)} all-to-all(bf16[4,32,768]{2,1,0:T(8,128)(2,1)} %get-tuple-element.20), channel_id=1, replica_groups=mesh['tower'=2,'y'=4,'x'=4,'zhi'=4,'head'=4] {'head'}, dimensions={0} | all-to-all | bytes 393216 | tf_op jit(solution)/shard_map/all_to_all | solution.py:144
  23.8 1.3 %broadcast_in_dim.10 = bf16[16,64,768]{2,1,0:T(8,128)(2,1)} broadcast(bf16[64,768]{1,0:T(8,128)(2,1)S(1)} %bitcast.12), dimensions={1,2} | broadcast | bytes 1671168 | tf_op jit(solution)/shard_map/broadcast_in_dim | solution.py:155
  25.1 0.0 copy-start.3
  25.1 4.4 %all-to-all-start.1 = ((bf16[16,64,768]{2,1,0:T(8,128)(2,1)}), bf16[16,64,768]{2,1,0:T(8,128)(2,1)S(1)}, u32[]{:S(2)}, u32[]{:S(2)}) async-start(bf16[16,64,768]{2,1,0:T(8,128)(2,1)} %broadcast_in_dim.10), calls=%async_computation.1 | async-start | bytes 3145728 | tf_op jit(solution)/shard_map/all_to_all | solution.py:156
  29.6 1.9 %collective-permute-start = (bf16[4,32,768]{2,1,0:T(8,128)(2,1)}, bf16[4,32,768]{2,1,0:T(8,128)(2,1)S(1)}, u32[]{:S(2)}, u32[]{:S(2)}) collective-permute-start(bf16[4,32,768]{2,1,0:T(8,128)(2,1)} %all_to_all.21), channel_id=1, source_target_pairs={{0,256},{4,260},{8,264},{12,268},{256,0},{260,4},{264,8},{268,12},... | collective-permute-start | bytes 589832 | tf_op jit(solution)/shard_map/ppermute | solution.py:152
  31.5 10.2 %collective-permute-start.1 = (bf16[4,32,768]{2,1,0:T(8,128)(2,1)}, bf16[4,32,768]{2,1,0:T(8,128)(2,1)S(1)}, u32[]{:S(2)}, u32[]{:S(2)}) collective-permute-start(bf16[4,32,768]{2,1,0:T(8,128)(2,1)} %all_to_all.21), channel_id=1, source_target_pairs={{4,256},{8,260},{12,264},{0,268},{260,0},{264,4},{268,8},{256,12},... | collective-permute-start | bytes 589832 | tf_op jit(solution)/shard_map/ppermute | solution.py:152
  41.7 5.9 %collective-permute-start.2 = (bf16[4,32,768]{2,1,0:T(8,128)(2,1)}, bf16[4,32,768]{2,1,0:T(8,128)(2,1)}, u32[]{:S(2)}, u32[]{:S(2)}) collective-permute-start(bf16[4,32,768]{2,1,0:T(8,128)(2,1)} %all_to_all.21), channel_id=1, source_target_pairs={{8,256},{12,260},{0,264},{4,268},{264,0},{268,4},{256,8},{260,12},... | collective-permute-start | bytes 589832 | tf_op jit(solution)/shard_map/ppermute | solution.py:152
  47.6 6.6 %collective-permute-start.3 = (bf16[4,32,768]{2,1,0:T(8,128)(2,1)}, bf16[4,32,768]{2,1,0:T(8,128)(2,1)}, u32[]{:S(2)}, u32[]{:S(2)}) collective-permute-start(bf16[4,32,768]{2,1,0:T(8,128)(2,1)} %all_to_all.21), channel_id=1, source_target_pairs={{12,256},{0,260},{4,264},{8,268},{268,0},{256,4},{260,8},{264,12},... | collective-permute-start | bytes 589832 | tf_op jit(solution)/shard_map/ppermute | solution.py:152
  54.2 0.0 copy-done.3
  54.2 0.7 fusion.3
  57.5 1.3 %stack.23.info_ref = s32[8]{0:T(128)S(1)} concatenate(s32[1]{0:T(128)} %bitcast, s32[1]{0:T(128)} %bitcast.1, s32[1]{0:T(128)} %bitcast.2, s32[1]{0:T(128)} %bitcast.3, s32[1]{0:T(128)} %bitcast.4, s32[1]{0:T(128)} %bitcast.5, s32[1]{0:T(128)} %bitcast.6, s32[1]{0:T(128)} %constant.65.clone.1), dimensions={0} | concatenate | bytes 64 | tf_op jit(solution)/shard_map/stack | solution.py:161
  58.8 0.0 collective-permute-done.refs_0_
  58.8 8.6 %collective-permute-done.1.refs_1_ = bf16[4,32,768]{2,1,0:T(8,128)(2,1)S(1)} collective-permute-done((bf16[4,32,768]{2,1,0:T(8,128)(2,1)}, bf16[4,32,768]{2,1,0:T(8,128)(2,1)S(1)}, u32[]{:S(2)}, u32[]{:S(2)}) %collective-permute-start.1) | collective-permute-done | bytes 196640 | tf_op jit(solution)/shard_map/ppermute | solution.py:152
  67.4 12.8 %collective-permute-done.2.refs_2_ = bf16[4,32,768]{2,1,0:T(8,128)(2,1)} collective-permute-done((bf16[4,32,768]{2,1,0:T(8,128)(2,1)}, bf16[4,32,768]{2,1,0:T(8,128)(2,1)}, u32[]{:S(2)}, u32[]{:S(2)}) %collective-permute-start.2) | collective-permute-done | bytes 196640 | tf_op jit(solution)/shard_map/ppermute | solution.py:152
  80.1 3.2 %collective-permute-done.3.refs_3_ = bf16[4,32,768]{2,1,0:T(8,128)(2,1)} collective-permute-done((bf16[4,32,768]{2,1,0:T(8,128)(2,1)}, bf16[4,32,768]{2,1,0:T(8,128)(2,1)}, u32[]{:S(2)}, u32[]{:S(2)}) %collective-permute-start.3) | collective-permute-done | bytes 196640 | tf_op jit(solution)/shard_map/ppermute | solution.py:152
  83.3 0.0 all-to-all-done.1.q_ref
  83.3 4.5 %attend.1 = bf16[16,64,896]{2,1,0:T(8,128)(2,1)S(1)} custom-call(s32[8]{0:T(128)S(1)} %stack.23.info_ref, bf16[16,64,768]{2,1,0:T(8,128)(2,1)S(1)} %all-to-all-done.1.q_ref, bf16[4,32,768]{2,1,0:T(8,128)(2,1)S(1)} %collective-permute-done.refs_0_, bf16[4,32,768]{2,1,0:T(8,128)(2,1)S(1)} %collective-permute-done.1.refs_1_, ...), custom_call_target="tpu_custom_call" | custom-call | tf_op jit(solution)/shard_map/attend/pallas_call | solution.py:179
  87.8 0.0 copy-start.1
  87.8 1.3 copy-done.1
  89.1 0.0 copy-start.4
  89.1 7.3 %all-to-all-start.3 = ((bf16[16,64,896]{2,1,0:T(8,128)(2,1)}), bf16[16,64,896]{2,1,0:T(8,128)(2,1)S(1)}, u32[]{:S(2)}, u32[]{:S(2)}) async-start(bf16[16,64,896]{2,1,0:T(8,128)(2,1)} %copy-done.1), calls=%async_computation.3 | async-start | bytes 3670016 | tf_op jit(solution)/shard_map/all_to_all | solution.py:187
  96.4 0.0 copy-start.2
  96.4 0.0 copy-done.4
  96.5 0.0 copy-done
  96.5 0.3 fusion.gates_ref
  96.8 28.1 %all-to-all-done.3.parts_ref = bf16[16,64,896]{2,1,0:T(8,128)(2,1)S(1)} async-done(((bf16[16,64,896]{2,1,0:T(8,128)(2,1)}), bf16[16,64,896]{2,1,0:T(8,128)(2,1)S(1)}, u32[]{:S(2)}, u32[]{:S(2)}) %all-to-all-start.3) | async-done | bytes 1835040 | tf_op jit(solution)/shard_map/all_to_all | solution.py:187
  124.9 0.0 copy-done.2
  124.9 2.4 %merge.1 = bf16[1,64,768]{2,1,0:T(8,128)(2,1)} custom-call(s32[8]{0:T(128)S(1)} %stack.23.info_ref, bf16[16,64,896]{2,1,0:T(8,128)(2,1)S(1)} %all-to-all-done.3.parts_ref, bf16[1,64,768]{2,1,0:T(8,128)(2,1)S(1)} %copy-done.2, f32[8,768]{1,0:T(8,128)S(1)} %fusion.gates_ref), custom_call_target="tpu_custom_call" | custom-call | tf_op jit(solution)/shard_map/merge/pallas_call | solution.py:188
  (2 shorter events, 0.0 us)
Async XLA Ops:
  0.0 96.5 %copy-start = (bf16[1,1000,768]{2,1,0:T(8,128)(2,1)S(1)}, bf16[1,1000,768]{2,1,0:T(8,128)(2,1)}, u32[]{:S(2)}) copy-start(bf16[1,1000,768]{2,1,0:T(8,128)(2,1)} %param.13) | copy-start | bytes 4608004
  25.1 29.1 %copy-start.3 = (s32[2,1,3]{2,1,0:T(1,128)S(1)}, s32[2,1,3]{2,1,0:T(1,128)}, u32[]{:S(2)}) copy-start(s32[2,1,3]{2,1,0:T(1,128)} %param.14) | copy-start | bytes 76
  25.1 58.2 %all-to-all-start.1 = ((bf16[16,64,768]{2,1,0:T(8,128)(2,1)}), bf16[16,64,768]{2,1,0:T(8,128)(2,1)S(1)}, u32[]{:S(2)}, u32[]{:S(2)}) async-start(bf16[16,64,768]{2,1,0:T(8,128)(2,1)} %broadcast_in_dim.10), calls=%async_computation.1 | async-start | bytes 3145728 | tf_op jit(solution)/shard_map/all_to_all | solution.py:156
  29.6 29.2 %collective-permute-start = (bf16[4,32,768]{2,1,0:T(8,128)(2,1)}, bf16[4,32,768]{2,1,0:T(8,128)(2,1)S(1)}, u32[]{:S(2)}, u32[]{:S(2)}) collective-permute-start(bf16[4,32,768]{2,1,0:T(8,128)(2,1)} %all_to_all.21), channel_id=1, source_target_pairs={{0,256},{4,260},{8,264},{12,268},{256,0},{260,4},{264,8},{268,12},... | collective-permute-start | bytes 589832 | tf_op jit(solution)/shard_map/ppermute | solution.py:152
  31.5 35.9 %collective-permute-start.1 = (bf16[4,32,768]{2,1,0:T(8,128)(2,1)}, bf16[4,32,768]{2,1,0:T(8,128)(2,1)S(1)}, u32[]{:S(2)}, u32[]{:S(2)}) collective-permute-start(bf16[4,32,768]{2,1,0:T(8,128)(2,1)} %all_to_all.21), channel_id=1, source_target_pairs={{4,256},{8,260},{12,264},{0,268},{260,0},{264,4},{268,8},{256,12},... | collective-permute-start | bytes 589832 | tf_op jit(solution)/shard_map/ppermute | solution.py:152
  41.7 38.4 %collective-permute-start.2 = (bf16[4,32,768]{2,1,0:T(8,128)(2,1)}, bf16[4,32,768]{2,1,0:T(8,128)(2,1)}, u32[]{:S(2)}, u32[]{:S(2)}) collective-permute-start(bf16[4,32,768]{2,1,0:T(8,128)(2,1)} %all_to_all.21), channel_id=1, source_target_pairs={{8,256},{12,260},{0,264},{4,268},{264,0},{268,4},{256,8},{260,12},... | collective-permute-start | bytes 589832 | tf_op jit(solution)/shard_map/ppermute | solution.py:152
  47.6 35.7 %collective-permute-start.3 = (bf16[4,32,768]{2,1,0:T(8,128)(2,1)}, bf16[4,32,768]{2,1,0:T(8,128)(2,1)}, u32[]{:S(2)}, u32[]{:S(2)}) collective-permute-start(bf16[4,32,768]{2,1,0:T(8,128)(2,1)} %all_to_all.21), channel_id=1, source_target_pairs={{12,256},{0,260},{4,264},{8,268},{268,0},{256,4},{260,8},{264,12},... | collective-permute-start | bytes 589832 | tf_op jit(solution)/shard_map/ppermute | solution.py:152
  87.8 1.3 %copy-start.1 = (bf16[16,64,896]{2,1,0:T(8,128)(2,1)}, bf16[16,64,896]{2,1,0:T(8,128)(2,1)S(1)}, u32[]{:S(2)}) copy-start(bf16[16,64,896]{2,1,0:T(8,128)(2,1)S(1)} %attend.1) | copy-start | bytes 5505028
  89.1 7.4 %copy-start.4 = (s32[1,3]{1,0:T(1,128)S(1)}, s32[1,3]{1,0:T(1,128)}, u32[]{:S(2)}) copy-start(s32[1,3]{1,0:T(1,128)} %param.15) | copy-start | bytes 40
  89.1 35.8 %all-to-all-start.3 = ((bf16[16,64,896]{2,1,0:T(8,128)(2,1)}), bf16[16,64,896]{2,1,0:T(8,128)(2,1)S(1)}, u32[]{:S(2)}, u32[]{:S(2)}) async-start(bf16[16,64,896]{2,1,0:T(8,128)(2,1)} %copy-done.1), calls=%async_computation.3 | async-start | bytes 3670016 | tf_op jit(solution)/shard_map/all_to_all | solution.py:187
  96.4 28.4 %copy-start.2 = (bf16[1,64,768]{2,1,0:T(8,128)(2,1)S(1)}, bf16[1,64,768]{2,1,0:T(8,128)(2,1)}, u32[]{:S(2)}) copy-start(bf16[1,64,768]{2,1,0:T(8,128)(2,1)} %hidden_ref.1) | copy-start | bytes 294916

commit v2 on v1

v2 whole, which is shorter than its diff:
```python
import functools

import jax
import jax.numpy as jnp
from jax import lax
from jax.experimental import pallas as pl
from jax.experimental.pallas import tpu as pltpu
from jax.sharding import Mesh, PartitionSpec as P

HEAD_DIM = 128
SCALE = HEAD_DIM**-0.5 * 1.4426950408889634
MASKED = -(2.0**100)
STATS = 128
SPLIT = 2
COLUMNS = ("yl", "x")


def sample_of(positions, bound_a, bound_b):
    return (positions >= bound_a).astype(jnp.int32) + (positions >= bound_b).astype(jnp.int32)


def bounds(lengths_ref, tower):
    first = lengths_ref[tower, 0, 0]
    return first, first + lengths_ref[tower, 0, 1]


def position(yh, yl, x, zhi, row, rows):
    column = (yh * lax.axis_size("yl") + yl) * lax.axis_size("x") + x
    return (column * lax.axis_size("zhi") + zhi) * rows + row


def pack_kernel(q_ref, k_ref, v_ref, out_ref):
    pairs, both, width = out_ref.shape
    halves = lax.axis_size("yh")
    groups, rows = pairs // (2 * halves), both // 2
    mine = lax.axis_index("tower") * (halves * groups)
    other = halves * groups - mine
    for s in range(halves):
        for g in range(groups):
            cols = slice((g * halves + s) * width, (g * halves + s + 1) * width)
            at = s * groups + g
            out_ref[mine + at, :rows] = q_ref[0, :, cols]
            out_ref[mine + at, rows:] = jnp.zeros((rows, width), jnp.bfloat16)
            out_ref[other + at, :rows] = k_ref[0, :, cols]
            out_ref[other + at, rows:] = v_ref[0, :, cols]


def copies_kernel(in_ref, q_ref, kv_ref):
    pairs, both, _ = in_ref.shape
    sources, rows = pairs // 2, both // 2
    mine = lax.axis_index("tower") * sources
    other = sources - mine
    for g in range(sources):
        q = in_ref[mine + g, :rows]
        k = in_ref[other + g, :rows]
        v = in_ref[other + g, rows:]
        for c in range(q_ref.shape[0]):
            q_ref[c, g * rows : (g + 1) * rows] = q
        for c in range(kv_ref.shape[0]):
            kv_ref[c, g * rows : (g + 1) * rows] = k
            kv_ref[c, (sources + g) * rows : (sources + g + 1) * rows] = v


def attend_kernel(lengths_ref, q_ref, kv_ref, out_ref):
    columns, part, width = q_ref.shape
    chunks = kv_ref.shape[0]
    heads = width // HEAD_DIM
    halves = lax.axis_size("yh")
    rows = part // halves
    keys = chunks * part
    tower = lax.axis_index("tower")
    yl, x, zhi = lax.axis_index("yl"), lax.axis_index("x"), lax.axis_index("zhi")
    own_a, own_b = bounds(lengths_ref, tower)
    far_a, far_b = bounds(lengths_ref, 1 - tower)

    lane = lax.broadcasted_iota(jnp.int32, (1, keys), 1)
    within = lane % part
    key_at = position(within // rows, yl, x, lane // part, within % rows, rows)
    key_ids = sample_of(key_at, far_a, far_b)
    stat_lane = lax.broadcasted_iota(jnp.int32, (1, STATS), 1)
    block = 2
    tile = block * part

    def step(t, _):
        r = lax.broadcasted_iota(jnp.int32, (tile, 1), 0)
        column, within = t * block + r // part, r % part
        query_at = position(
            within // rows,
            column // lax.axis_size("x"),
            column % lax.axis_size("x"),
            zhi,
            within % rows,
            rows,
        )
        allowed = sample_of(query_at, own_a, own_b) == key_ids
        stats = jnp.zeros((tile, STATS), jnp.float32)
        for h in range(heads):
            cols = slice(h * HEAD_DIM, (h + 1) * HEAD_DIM)
            q = q_ref[pl.ds(t * block, block), :, cols].reshape(tile, HEAD_DIM)
            k = kv_ref[:, :part, cols].reshape(keys, HEAD_DIM)
            v = kv_ref[:, part:, cols].reshape(keys, HEAD_DIM)
            v = jnp.concatenate([v, jnp.ones((keys, HEAD_DIM), v.dtype)], axis=1)
            s = lax.dot_general(q, k, (((1,), (1,)), ((), ())), preferred_element_type=jnp.float32)
            s = jnp.where(allowed, s * SCALE, MASKED)
            top = jnp.max(s, axis=1, keepdims=True).astype(jnp.bfloat16).astype(jnp.float32)
            p = jnp.exp2(s - top).astype(jnp.bfloat16)
            o = jnp.dot(p, v, preferred_element_type=jnp.float32)
            total = o[:, HEAD_DIM:]
            high = total.astype(jnp.bfloat16).astype(jnp.float32)
            stats = jnp.where(stat_lane == h, top, stats)
            stats = jnp.where(stat_lane == 32 + h, high, stats)
            stats = jnp.where(stat_lane == 64 + h, total - high, stats)
            o = o[:, :HEAD_DIM].astype(jnp.bfloat16).reshape(block, halves, rows, HEAD_DIM)
            for s2 in range(halves):
                out_ref[s2, pl.ds(t * block, block), :, cols] = o[:, s2]
        stats = stats.astype(jnp.bfloat16).reshape(block, halves, rows, STATS)
        for s2 in range(halves):
            out_ref[s2, pl.ds(t * block, block), :, width:] = stats[:, s2]
        return 0

    lax.fori_loop(0, columns // block, step, 0)


def merge_kernel(lengths_ref, steps_ref, parts_ref, hidden_ref, table_ref, out_ref):
    halves, columns, rows, full = parts_ref.shape
    width = full - STATS
    heads = width // HEAD_DIM
    own_a, own_b = bounds(lengths_ref, lax.axis_index("tower"))
    yh, yl, x = lax.axis_index("yh"), lax.axis_index("yl"), lax.axis_index("x")
    row = lax.broadcasted_iota(jnp.int32, (rows, 1), 0)
    ids = sample_of(position(yh, yl, x, lax.axis_index("zhi"), row, rows), own_a, own_b)
    row_steps = jnp.where(
        ids == 0, steps_ref[0, 0], jnp.where(ids == 1, steps_ref[0, 1], steps_ref[0, 2])
    )
    chosen = row_steps == lax.broadcasted_iota(jnp.int32, (1, table_ref.shape[1]), 1)
    chosen = jnp.where(chosen, 1.0, 0.0).astype(jnp.bfloat16)
    gates = jnp.dot(chosen, table_ref[0], preferred_element_type=jnp.float32)
    for s2 in range(halves):
        stats = [parts_ref[s2, j, :, width:].astype(jnp.float32) for j in range(columns)]
        top = functools.reduce(jnp.maximum, stats)
        scales, total = [], jnp.zeros_like(top)
        for st in stats:
            scale = jnp.exp2(jnp.minimum(st - top, 0.0))
            sums = pltpu.roll(st, STATS - 32, 1) + pltpu.roll(st, STATS - 64, 1)
            scales.append(scale)
            total = total + scale * sums
        inverse = 1.0 / total
        scales = [scale * inverse for scale in scales]
        for h in range(heads):
            cols = slice(h * HEAD_DIM, (h + 1) * HEAD_DIM)
            o = jnp.zeros((rows, HEAD_DIM), jnp.float32)
            for j in range(columns):
                part = parts_ref[s2, j, :, cols].astype(jnp.float32)
                o = o + scales[j][:, h : h + 1] * part
            cols = slice(s2 * width + h * HEAD_DIM, s2 * width + (h + 1) * HEAD_DIM)
            out_ref[0, :, cols] = (
                hidden_ref[0, :, cols].astype(jnp.float32) + gates[:, cols] * o
            ).astype(jnp.bfloat16)


def vmem(n):
    return [pl.BlockSpec(memory_space=pltpu.VMEM)] * n


SMEM = pl.BlockSpec(memory_space=pltpu.SMEM)
PARAMS = pltpu.CompilerParams(vmem_limit_bytes=40 * 1024 * 1024)


def shards(queries, key_rows, value_rows, hidden, gate_table, lengths, step_ids):
    groups = lax.axis_size("head")
    halves = lax.axis_size("yh")
    columns = lax.axis_size(COLUMNS)
    chunks = lax.axis_size("zhi")
    rows, width = queries.shape[1], queries.shape[2] // (groups * halves)
    part = rows * groups * halves

    sent = pl.pallas_call(
        pack_kernel,
        out_shape=jax.ShapeDtypeStruct((2 * halves * groups, 2 * rows, width), jnp.bfloat16),
        in_specs=vmem(3),
        out_specs=vmem(1)[0],
        name="pack",
    )(queries, key_rows, value_rows)
    sent = lax.all_to_all(sent, ("tower", "yh", "head"), 0, 0, tiled=True)
    qs, kv = pl.pallas_call(
        copies_kernel,
        out_shape=(
            jax.ShapeDtypeStruct((columns, part, width), jnp.bfloat16),
            jax.ShapeDtypeStruct((1, 2 * part, width), jnp.bfloat16),
        ),
        in_specs=vmem(1),
        out_specs=tuple(vmem(2)),
        compiler_params=PARAMS,
        name="copies",
    )(sent)
    qs = lax.all_to_all(qs, COLUMNS, 0, 0, tiled=True)
    kv = lax.all_gather(kv[0], "zhi", axis=0, tiled=True).reshape(chunks, 2 * part, width)

    parts = pl.pallas_call(
        attend_kernel,
        out_shape=jax.ShapeDtypeStruct(
            (halves, columns, part // halves, width + STATS), jnp.bfloat16
        ),
        in_specs=[SMEM] + vmem(2),
        out_specs=vmem(1)[0],
        compiler_params=PARAMS,
        name="attend",
    )(lengths, qs, kv)
    parts, hidden, gate_table = lax.optimization_barrier((parts, hidden, gate_table))
    shape = parts.shape
    parts = lax.all_to_all(
        parts.reshape((halves * columns,) + shape[2:]), ("yh",) + COLUMNS, 0, 0, tiled=True
    )
    return pl.pallas_call(
        merge_kernel,
        out_shape=jax.ShapeDtypeStruct(hidden.shape, jnp.bfloat16),
        in_specs=[SMEM, SMEM] + vmem(3),
        out_specs=vmem(1)[0],
        compiler_params=PARAMS,
        name="merge",
    )(lengths, step_ids, parts.reshape(shape), hidden, gate_table)


def solution(mesh):
    towers, seq, head = mesh.devices.shape
    fine = Mesh(
        mesh.devices.reshape(towers, SPLIT, 4 // SPLIT, 4, seq // 16, head),
        ("tower", "yh", "yl", "x", "zhi", "head"),
    )
    seq_axes = ("yh", "yl", "x", "zhi")
    rows = P("tower", seq_axes + ("head",), None)
    block = P("tower", seq_axes, "head")
    return jax.shard_map(
        shards,
        mesh=fine,
        in_specs=(rows, rows, rows, block, P("tower", None, "head"), P(), P()),
        out_specs=block,
        check_vma=False,
    )
```

time: 128 us -> 98.3 us (0.77)
  the two profiles are of different devices: /device:TPU:96 before, /device:TPU:1 now
where the time goes in v2:
time: 98.3 us; the launch traced here: 97.9 us
  blocking collectives  84.8 us (86%)
  Pallas kernels  9.15 us (9%)
  starting transfers between devices  3.92 us (4%)
    all_gather x1, blocking collectives, shards(): lax.all_gather(kv[0], 'zhi', axis=0, tiled=True)  38.4 us
    all_to_all x1, blocking collectives, shards(): sent = lax.all_to_all(sent, ('tower', 'yh', 'head'), 0, 0, tiled=True)  24.5 us
    all_to_all x1, blocking collectives, shards(): lax.all_to_all(parts.reshape((halves * columns,) + shape[2:]), ('yh',) +...  21.9 us
    pallas_call x1, Pallas kernels, shards(): pl.pallas_call(attend_kernel, out_shape=jax.ShapeDtypeStruct((halves, col...  4.22 us
    all_to_all x1, starting transfers between devices, shards(): qs = lax.all_to_all(qs, COLUMNS, 0, 0, tiled=True)  3.92 us
    pallas_call x1, Pallas kernels, shards(): pl.pallas_call(merge_kernel, out_shape=jax.ShapeDtypeStruct(hidden.shape,...  2.17 us
  transfers between devices with their start and end apart: 1, of which 0 were waited for; matrix products, arithmetic and copies ran while one was open for 0% of the time, Pallas kernels for 0%

profile of v2, /device:TPU:1, one launch (start us, length us, event | category | flops | bytes accessed | tf_op | source)
XLA Modules:
  0.0 97.9 jit_solution(1200239029213228376)
XLA Ops:
  0.0 1.8 %pack.1 = bf16[16,32,384]{2,1,0:T(8,128)(2,1)} custom-call(bf16[1,16,3072]{2,1,0:T(8,128)(2,1)} %q_ref.1, bf16[1,16,3072]{2,1,0:T(8,128)(2,1)} %k_ref.1, bf16[1,16,3072]{2,1,0:T(8,128)(2,1)} %v_ref.1), custom_call_target="tpu_custom_call" | custom-call | tf_op jit(solution)/shard_map/pack/pallas_call | solution.py:177
  1.8 24.5 %all_to_all.15.in_ref = bf16[16,32,384]{2,1,0:T(8,128)(2,1)S(1)} all-to-all(bf16[16,32,384]{2,1,0:T(8,128)(2,1)} %pack.1), channel_id=1, replica_groups=mesh['tower'=2,'yh'=2,'yl'=2,'x'=4,'zhi'=4,'head'=4] {'tower','yh','head'}, dimensions={0} | all-to-all | bytes 786432 | tf_op jit(solution)/shard_map/all_to_all | solution.py:184
  26.3 0.0 copy-start.2
  26.3 1.0 copies.1
  27.3 3.9 %all-to-all-start.1 = ((bf16[8,128,384]{2,1,0:T(8,128)(2,1)}), bf16[8,128,384]{2,1,0:T(8,128)(2,1)S(1)}, u32[]{:S(2)}, u32[]{:S(2)}) async-start(bf16[8,128,384]{2,1,0:T(8,128)(2,1)} %get-tuple-element.10), calls=%async_computation.1 | async-start | bytes 1572864 | tf_op jit(solution)/shard_map/all_to_all | solution.py:196
  31.2 38.4 %all-gather = bf16[1,1024,384]{2,1,0:T(8,128)(2,1)S(1)} all-gather(bf16[1,256,384]{2,1,0:T(8,128)(2,1)S(1)} %get-tuple-element.11), channel_id=2, replica_groups=mesh['tower'=2,'yh'=2,'yl'=2,'x'=4,'zhi'=4,'head'=4] {'zhi'}, dimensions={1}, use_global_device_ids=true | all-gather | bytes 983040 | tf_op jit(solution)/shard_map/all_gather | solution.py:197
  69.6 0.0 all-to-all-done.1.q_ref
  69.6 0.0 copy-done.2
  69.6 4.2 %attend.1 = bf16[2,8,64,512]{3,2,1,0:T(8,128)(2,1)S(1)} custom-call(s32[2,1,3]{2,1,0:T(1,128)S(1)} %copy-done.2, bf16[8,128,384]{2,1,0:T(8,128)(2,1)S(1)} %all-to-all-done.1.q_ref, bf16[4,256,384]{2,1,0:T(8,128)(2,1)S(1)} %bitcast.5), custom_call_target="tpu_custom_call" | custom-call | tf_op jit(solution)/shard_map/attend/pallas_call | solution.py:199
  73.8 0.0 copy-start
  73.8 0.0 copy-start.1
  73.8 0.0 copy-start.3
  73.9 21.9 %all_to_all.16 = bf16[16,64,512]{2,1,0:T(8,128)(2,1)S(1)} all-to-all(bf16[16,64,512]{2,1,0:T(8,128)(2,1)S(1)} %bitcast.3), channel_id=1, replica_groups=mesh['tower'=2,'yh'=2,'yl'=2,'x'=4,'zhi'=4,'head'=4] {'yh','yl','x'}, dimensions={0} | all-to-all | bytes 2097152 | tf_op jit(solution)/shard_map/all_to_all | solution.py:211
  95.7 0.0 copy-done
  95.7 0.0 copy-done.1
  95.7 0.0 copy-done.3
  95.7 2.2 %merge.1 = bf16[1,64,768]{2,1,0:T(8,128)(2,1)} custom-call(s32[2,1,3]{2,1,0:T(1,128)S(1)} %copy-done.2, s32[1,3]{1,0:T(1,128)S(1)} %copy-done.3, bf16[2,8,64,512]{3,2,1,0:T(8,128)(2,1)S(1)} %bitcast.4, bf16[1,64,768]{2,1,0:T(8,128)(2,1)S(1)} %copy-done.1, bf16[1,1000,768]{2,1,0:T(8,128)(2,1)S(1)} %copy-done), custom_call_target="tpu_custom_call" | custom-call | tf_op jit(solution)/shard_map/merge/pallas_call | solution.py:214
Async XLA Ops:
  26.3 43.3 %copy-start.2 = (s32[2,1,3]{2,1,0:T(1,128)S(1)}, s32[2,1,3]{2,1,0:T(1,128)}, u32[]{:S(2)}) copy-start(s32[2,1,3]{2,1,0:T(1,128)} %lengths_ref.3) | copy-start | bytes 76
  27.3 42.3 %all-to-all-start.1 = ((bf16[8,128,384]{2,1,0:T(8,128)(2,1)}), bf16[8,128,384]{2,1,0:T(8,128)(2,1)S(1)}, u32[]{:S(2)}, u32[]{:S(2)}) async-start(bf16[8,128,384]{2,1,0:T(8,128)(2,1)} %get-tuple-element.10), calls=%async_computation.1 | async-start | bytes 1572864 | tf_op jit(solution)/shard_map/all_to_all | solution.py:196
  73.8 21.9 %copy-start = (bf16[1,1000,768]{2,1,0:T(8,128)(2,1)S(1)}, bf16[1,1000,768]{2,1,0:T(8,128)(2,1)}, u32[]{:S(2)}) copy-start(bf16[1,1000,768]{2,1,0:T(8,128)(2,1)} %table_ref) | copy-start | bytes 4608004
  73.8 21.9 %copy-start.1 = (bf16[1,64,768]{2,1,0:T(8,128)(2,1)S(1)}, bf16[1,64,768]{2,1,0:T(8,128)(2,1)}, u32[]{:S(2)}) copy-start(bf16[1,64,768]{2,1,0:T(8,128)(2,1)} %hidden_ref) | copy-start | bytes 294916
  73.8 21.9 %copy-start.3 = (s32[1,3]{1,0:T(1,128)S(1)}, s32[1,3]{1,0:T(1,128)}, u32[]{:S(2)}) copy-start(s32[1,3]{1,0:T(1,128)} %steps_ref.1) | copy-start | bytes 40

commit v3 on v2

v3 whole, which is shorter than its diff:
```python
import functools

import jax
import jax.numpy as jnp
from jax import lax
from jax.experimental import pallas as pl
from jax.experimental.pallas import tpu as pltpu
from jax.sharding import Mesh, PartitionSpec as P

HEAD_DIM = 128
SCALE = HEAD_DIM**-0.5 * 1.4426950408889634
MASKED = -(2.0**100)
STATS = 16
SPLIT = 2
COLUMNS = ("yl", "x")


def sample_of(positions, bound_a, bound_b):
    return (positions >= bound_a).astype(jnp.int32) + (positions >= bound_b).astype(jnp.int32)


def bounds(lengths_ref, tower):
    first = lengths_ref[tower, 0, 0]
    return first, first + lengths_ref[tower, 0, 1]


def position(yh, yl, x, zhi, row, rows):
    column = (yl * lax.axis_size("yh") + yh) * lax.axis_size("x") + x
    return (column * lax.axis_size("zhi") + zhi) * rows + row


def pack_kernel(q_ref, k_ref, v_ref, out_ref):
    pairs, triple, width = out_ref.shape
    halves = lax.axis_size("yh")
    groups, rows = pairs // halves, triple // 3
    for i, ref in enumerate((q_ref, k_ref, v_ref)):
        for s in range(halves):
            for g in range(groups):
                cols = slice((g * halves + s) * width, (g * halves + s + 1) * width)
                out_ref[s * groups + g, i * rows : (i + 1) * rows] = ref[0, :, cols]


def copies_kernel(in_ref, q_ref, kv_ref):
    sources, triple, _ = in_ref.shape[1:]
    rows = triple // 3
    mine = lax.axis_index("tower")
    other = 1 - mine
    for g in range(sources):
        q = in_ref[mine, g, :rows]
        for c in range(q_ref.shape[0]):
            q_ref[c, g * rows : (g + 1) * rows] = q
        kv_ref[g * rows : (g + 1) * rows] = in_ref[other, g, rows : 2 * rows]
        kv_ref[(sources + g) * rows : (sources + g + 1) * rows] = in_ref[other, g, 2 * rows :]


def attend_kernel(lengths_ref, q_ref, kv_ref, out_ref):
    columns, part, width = q_ref.shape
    chunks = kv_ref.shape[0]
    heads = width // HEAD_DIM
    halves = lax.axis_size("yh")
    rows = part // halves
    keys = chunks * part
    tower = lax.axis_index("tower")
    yl, x, zhi = lax.axis_index("yl"), lax.axis_index("x"), lax.axis_index("zhi")
    own_a, own_b = bounds(lengths_ref, tower)
    far_a, far_b = bounds(lengths_ref, 1 - tower)

    lane = lax.broadcasted_iota(jnp.int32, (1, keys), 1)
    within = lane % part
    key_ids = sample_of(
        position(within // rows, yl, x, lane // part, within % rows, rows), far_a, far_b
    )
    lane = lax.broadcasted_iota(jnp.int32, (1, HEAD_DIM), 1)
    block = columns
    tile = block * part

    def step(t, _):
        r = lax.broadcasted_iota(jnp.int32, (tile, 1), 0)
        column, within = t * block + r // part, r % part
        query_at = position(
            within // rows,
            column // lax.axis_size("x"),
            column % lax.axis_size("x"),
            zhi,
            within % rows,
            rows,
        )
        allowed = sample_of(query_at, own_a, own_b) == key_ids
        stats = jnp.zeros((tile, HEAD_DIM), jnp.float32)
        for h in range(heads):
            cols = slice(h * HEAD_DIM, (h + 1) * HEAD_DIM)
            q = q_ref[pl.ds(t * block, block), :, cols].reshape(tile, HEAD_DIM)
            k = kv_ref[:, :part, cols].reshape(keys, HEAD_DIM)
            v = kv_ref[:, part:, cols].reshape(keys, HEAD_DIM)
            s = lax.dot_general(q, k, (((1,), (1,)), ((), ())), preferred_element_type=jnp.float32)
            s = jnp.where(allowed, s, MASKED)
            top = (jnp.max(s, axis=1, keepdims=True) * SCALE).astype(jnp.bfloat16)
            top = top.astype(jnp.float32)
            empty = top < 0.01 * MASKED
            shift = jnp.where(empty, 0.0, top)
            p = jnp.exp2(s * SCALE - shift)
            total = jnp.sum(p, axis=1, keepdims=True)
            o = jnp.dot(p.astype(jnp.bfloat16), v, preferred_element_type=jnp.float32)
            high = total.astype(jnp.bfloat16).astype(jnp.float32)
            stats = jnp.where(lane == h, jnp.where(empty, MASKED, top), stats)
            stats = jnp.where(lane == 4 + h, total - high, stats)
            stats = jnp.where(lane == 8 + h, high, stats)
            o = o.astype(jnp.bfloat16).reshape(block, halves, rows, HEAD_DIM)
            for s2 in range(halves):
                out_ref[s2, pl.ds(t * block, block), h * rows : (h + 1) * rows, :] = o[:, s2]
        pick = lax.broadcasted_iota(jnp.int32, (STATS, 1), 0) == lane
        stats = lax.dot_general(
            jnp.where(pick, 1.0, 0.0).astype(jnp.bfloat16),
            stats.astype(jnp.bfloat16),
            (((1,), (1,)), ((), ())),
            preferred_element_type=jnp.float32,
        ).astype(jnp.bfloat16)
        for c in range(block):
            for s2 in range(halves):
                at = (c * halves + s2) * rows
                out_ref[s2, t * block + c, heads * rows :, :rows] = stats[:, at : at + rows]
                out_ref[s2, t * block + c, heads * rows :, rows:] = jnp.zeros(
                    (STATS, HEAD_DIM - rows), jnp.bfloat16
                )
        return 0

    lax.fori_loop(0, columns // block, step, 0)


def merge_kernel(lengths_ref, steps_ref, parts_ref, hidden_ref, table_ref, out_ref):
    halves, columns, full, _ = parts_ref.shape
    rows = hidden_ref.shape[1]
    heads = (full - STATS) // rows
    own_a, own_b = bounds(lengths_ref, lax.axis_index("tower"))
    yh, yl, x = lax.axis_index("yh"), lax.axis_index("yl"), lax.axis_index("x")
    row = lax.broadcasted_iota(jnp.int32, (rows, 1), 0)
    ids = sample_of(position(yh, yl, x, lax.axis_index("zhi"), row, rows), own_a, own_b)

    gates = []
    for i in range(3):
        wanted = steps_ref[0, i]
        eight = table_ref[wanted // 8].astype(jnp.float32)
        found = lax.broadcasted_iota(jnp.int32, (8, 1), 0) == wanted % 8
        gates.append(jnp.sum(jnp.where(found, eight, 0.0), axis=0, keepdims=True))

    scales = []
    for s2 in range(halves):
        stats = [parts_ref[s2, j, heads * rows :, :].astype(jnp.float32) for j in range(columns)]
        tops = [st[:8] for st in stats]
        top = functools.reduce(jnp.maximum, tops)
        factors, total = [], jnp.zeros_like(top)
        for st in stats:
            factor = jnp.exp2(jnp.minimum(st[:8] - top, 0.0))
            sums = st[8:] + jnp.concatenate([st[4:8], st[:4]], axis=0)
            factors.append(factor)
            total = total + factor * sums
        inverse = 1.0 / jnp.where(total > 0.0, total, 1.0)
        scales += [factor * inverse for factor in factors]
    scales = jnp.concatenate(scales, axis=0).T
    for s2 in range(halves):
        for h in range(heads):
            o = jnp.zeros((rows, HEAD_DIM), jnp.float32)
            for j in range(columns):
                part = parts_ref[s2, j, h * rows : (h + 1) * rows, :].astype(jnp.float32)
                at = (s2 * columns + j) * 8 + h
                o = o + scales[:rows, at : at + 1] * part
            cols = slice((s2 * heads + h) * HEAD_DIM, (s2 * heads + h + 1) * HEAD_DIM)
            gate = jnp.where(
                ids == 0, gates[0][:, cols], jnp.where(ids == 1, gates[1][:, cols], gates[2][:, cols])
            )
            out_ref[0, :, cols] = (hidden_ref[0, :, cols].astype(jnp.float32) + gate * o).astype(
                jnp.bfloat16
            )


def vmem(n):
    return [pl.BlockSpec(memory_space=pltpu.VMEM)] * n


SMEM = pl.BlockSpec(memory_space=pltpu.SMEM)
HBM = pl.BlockSpec(memory_space=pltpu.HBM)


def params(mib):
    return pltpu.CompilerParams(vmem_limit_bytes=mib * 1024 * 1024)


def shards(queries, key_rows, value_rows, hidden, gate_table, lengths, step_ids):
    groups = lax.axis_size("head")
    halves = lax.axis_size("yh")
    columns = lax.axis_size(COLUMNS)
    chunks = lax.axis_size("zhi")
    rows, width = queries.shape[1], queries.shape[2] // (groups * halves)
    heads = width // HEAD_DIM
    part = rows * groups * halves

    sent = pl.pallas_call(
        pack_kernel,
        out_shape=jax.ShapeDtypeStruct((halves * groups, 3 * rows, width), jnp.bfloat16),
        in_specs=vmem(3),
        out_specs=vmem(1)[0],
        compiler_params=params(60),
        name="pack",
    )(queries, key_rows, value_rows)
    sent = lax.all_to_all(sent, ("yh", "head"), 0, 0, tiled=True)
    sent = lax.all_gather(sent, "tower", axis=0, tiled=False)
    qs, kv = pl.pallas_call(
        copies_kernel,
        out_shape=(
            jax.ShapeDtypeStruct((columns, part, width), jnp.bfloat16),
            jax.ShapeDtypeStruct((2 * part, width), jnp.bfloat16),
        ),
        in_specs=vmem(1),
        out_specs=tuple(vmem(2)),
        compiler_params=params(8),
        name="copies",
    )(sent)
    qs = lax.all_to_all(qs, COLUMNS, 0, 0, tiled=True)
    kv = lax.all_gather(kv, "zhi", axis=0, tiled=True).reshape(chunks, 2 * part, width)

    shape = (halves, columns, heads * (part // halves) + STATS, HEAD_DIM)
    parts = pl.pallas_call(
        attend_kernel,
        out_shape=jax.ShapeDtypeStruct(shape, jnp.bfloat16),
        in_specs=[SMEM] + vmem(2),
        out_specs=vmem(1)[0],
        compiler_params=params(24),
        name="attend",
    )(lengths, qs, kv)
    parts, hidden, gate_table = lax.optimization_barrier((parts, hidden, gate_table))
    parts = lax.all_to_all(
        parts.reshape((halves * columns,) + shape[2:]), ("yh",) + COLUMNS, 0, 0, tiled=True
    )
    return pl.pallas_call(
        merge_kernel,
        out_shape=jax.ShapeDtypeStruct(hidden.shape, jnp.bfloat16),
        in_specs=[SMEM, SMEM] + vmem(3),
        out_specs=vmem(1)[0],
        compiler_params=params(16),
        name="merge",
    )(
        lengths,
        step_ids,
        parts.reshape(shape),
        hidden,
        gate_table.reshape(gate_table.shape[1] // 8, 8, gate_table.shape[2]),
    )


def solution(mesh):
    towers, seq, head = mesh.devices.shape
    fine = Mesh(
        mesh.devices.reshape(towers, 4 // SPLIT, SPLIT, 4, seq // 16, head),
        ("tower", "yl", "yh", "x", "zhi", "head"),
    )
    seq_axes = ("yl", "yh", "x", "zhi")
    rows = P("tower", seq_axes + ("head",), None)
    block = P("tower", seq_axes, "head")
    return jax.shard_map(
        shards,
        mesh=fine,
        in_specs=(rows, rows, rows, block, P("tower", None, "head"), P(), P()),
        out_specs=block,
        check_vma=False,
    )
```

time: 98.3 us -> 94.8 us (0.964)
  the two profiles are of different devices: /device:TPU:1 before, /device:TPU:2 now
where the time goes in v3:
time: 94.8 us; the launch traced here: 94.5 us
  blocking collectives  79 us (83%)
  Pallas kernels  8.32 us (9%)
  starting transfers between devices  7.17 us (8%)
    all_gather x1, blocking collectives, shards(): lax.all_gather(kv, 'zhi', axis=0, tiled=True)  41.5 us
    all_to_all x1, blocking collectives, shards(): lax.all_to_all(parts.reshape((halves * columns,) + shape[2:]), ('yh',) +...  17.9 us
    all_to_all x1, blocking collectives, shards(): sent = lax.all_to_all(sent, ('yh', 'head'), 0, 0, tiled=True)  17.4 us
    all_to_all x1, starting transfers between devices, shards(): qs = lax.all_to_all(qs, COLUMNS, 0, 0, tiled=True)  7.17 us
    pallas_call x1, Pallas kernels, shards(): pl.pallas_call(attend_kernel, out_shape=jax.ShapeDtypeStruct(shape, jnp.b...  3.72 us
    all_gather x1, blocking collectives, shards(): sent = lax.all_gather(sent, 'tower', axis=0, tiled=False)  2.22 us
    pallas_call x1, Pallas kernels, shards(): pl.pallas_call(merge_kernel, out_shape=jax.ShapeDtypeStruct(hidden.shape,...  1.9 us
  transfers between devices with their start and end apart: 1, of which 0 were waited for; matrix products, arithmetic and copies ran while one was open for 0% of the time, Pallas kernels for 0%

profile of v3, /device:TPU:2, one launch (start us, length us, event | category | flops | bytes accessed | tf_op | source)
XLA Modules:
  0.0 94.5 jit_solution(9765427318969487197)
XLA Ops:
  0.0 1.7 %pack.1 = bf16[8,48,384]{2,1,0:T(8,128)(2,1)} custom-call(bf16[1,16,3072]{2,1,0:T(8,128)(2,1)} %q_ref.1, bf16[1,16,3072]{2,1,0:T(8,128)(2,1)} %k_ref.1, bf16[1,16,3072]{2,1,0:T(8,128)(2,1)} %v_ref.1), custom_call_target="tpu_custom_call" | custom-call | tf_op jit(solution)/shard_map/pack/pallas_call | solution.py:197
  1.7 17.4 %all_to_all.15 = bf16[8,48,384]{2,1,0:T(8,128)(2,1)S(1)} all-to-all(bf16[8,48,384]{2,1,0:T(8,128)(2,1)} %pack.1), channel_id=1, replica_groups=mesh['tower'=2,'yl'=2,'yh'=2,'x'=4,'zhi'=4,'head'=4] {'yh','head'}, dimensions={0} | all-to-all | bytes 589824 | tf_op jit(solution)/shard_map/all_to_all | solution.py:205
  19.1 2.2 %all-gather = bf16[16,48,384]{2,1,0:T(8,128)(2,1)S(1)} all-gather(bf16[8,48,384]{2,1,0:T(8,128)(2,1)S(1)} %all_to_all.15), channel_id=2, replica_groups=mesh['tower'=2,'yl'=2,'yh'=2,'x'=4,'zhi'=4,'head'=4] {'tower'}, dimensions={0}, use_global_device_ids=true | all-gather | bytes 884736 | tf_op jit(solution)/shard_map/all_gather | solution.py:206
  21.3 0.0 copy-start.2
  21.3 1.0 %copies.1 = (bf16[8,128,384]{2,1,0:T(8,128)(2,1)}, bf16[256,384]{1,0:T(8,128)(2,1)S(1)}) custom-call(bf16[2,8,48,384]{3,2,1,0:T(8,128)(2,1)S(1)} %bitcast.8), custom_call_target="tpu_custom_call" | custom-call | tf_op jit(solution)/shard_map/copies/pallas_call | solution.py:207
  22.3 7.2 %all-to-all-start.1 = ((bf16[8,128,384]{2,1,0:T(8,128)(2,1)}), bf16[8,128,384]{2,1,0:T(8,128)(2,1)S(1)}, u32[]{:S(2)}, u32[]{:S(2)}) async-start(bf16[8,128,384]{2,1,0:T(8,128)(2,1)} %get-tuple-element.10), calls=%async_computation.1 | async-start | bytes 1572864 | tf_op jit(solution)/shard_map/all_to_all | solution.py:218
  29.5 41.5 %all_gather.11 = bf16[1024,384]{1,0:T(8,128)(2,1)S(1)} all-gather(bf16[256,384]{1,0:T(8,128)(2,1)S(1)} %get-tuple-element.11), channel_id=1, replica_groups=mesh['tower'=2,'yl'=2,'yh'=2,'x'=4,'zhi'=4,'head'=4] {'zhi'}, dimensions={0}, use_global_device_ids=true | all-gather | bytes 983040 | tf_op jit(solution)/shard_map/all_gather | solution.py:219
  71.0 0.0 all-to-all-done.1.q_ref
  71.0 0.0 copy-done.2
  71.0 0.0 copy-start
  71.0 0.0 copy-start.1
  71.0 0.0 copy-start.3
  71.0 3.7 %attend.1 = bf16[2,8,208,128]{3,2,1,0:T(8,128)(2,1)S(1)} custom-call(s32[2,1,3]{2,1,0:T(1,128)S(1)} %copy-done.2, bf16[8,128,384]{2,1,0:T(8,128)(2,1)S(1)} %all-to-all-done.1.q_ref, bf16[4,256,384]{2,1,0:T(8,128)(2,1)S(1)} %bitcast.7), custom_call_target="tpu_custom_call" | custom-call | tf_op jit(solution)/shard_map/attend/pallas_call | solution.py:222
  74.7 17.9 %all_to_all.16 = bf16[16,208,128]{2,1,0:T(8,128)(2,1)S(1)} all-to-all(bf16[16,208,128]{2,1,0:T(8,128)(2,1)S(1)} %bitcast.5), channel_id=1, replica_groups=mesh['tower'=2,'yl'=2,'yh'=2,'x'=4,'zhi'=4,'head'=4] {'yh','yl','x'}, dimensions={0} | all-to-all | bytes 1703936 | tf_op jit(solution)/shard_map/all_to_all | solution.py:231
  92.6 0.0 copy-done
  92.6 0.0 copy-done.1
  92.6 0.0 copy-done.3
  92.6 1.9 %merge.1 = bf16[1,64,768]{2,1,0:T(8,128)(2,1)} custom-call(s32[2,1,3]{2,1,0:T(1,128)S(1)} %copy-done.2, s32[1,3]{1,0:T(1,128)S(1)} %copy-done.3, bf16[2,8,208,128]{3,2,1,0:T(8,128)(2,1)S(1)} %bitcast.6, bf16[1,64,768]{2,1,0:T(8,128)(2,1)S(1)} %copy-done.1, bf16[125,8,768]{2,1,0:T(8,128)(2,1)S(1)} %bitcast.9), custom_call_target="tpu_custom_call" | custom-call | tf_op jit(solution)/shard_map/merge/pallas_call | solution.py:234
Async XLA Ops:
  21.3 49.7 %copy-start.2 = (s32[2,1,3]{2,1,0:T(1,128)S(1)}, s32[2,1,3]{2,1,0:T(1,128)}, u32[]{:S(2)}) copy-start(s32[2,1,3]{2,1,0:T(1,128)} %lengths_ref.3) | copy-start | bytes 76
  22.3 48.7 %all-to-all-start.1 = ((bf16[8,128,384]{2,1,0:T(8,128)(2,1)}), bf16[8,128,384]{2,1,0:T(8,128)(2,1)S(1)}, u32[]{:S(2)}, u32[]{:S(2)}) async-start(bf16[8,128,384]{2,1,0:T(8,128)(2,1)} %get-tuple-element.10), calls=%async_computation.1 | async-start | bytes 1572864 | tf_op jit(solution)/shard_map/all_to_all | solution.py:218
  71.0 21.6 %copy-start = (bf16[1,1000,768]{2,1,0:T(8,128)(2,1)S(1)}, bf16[1,1000,768]{2,1,0:T(8,128)(2,1)}, u32[]{:S(2)}) copy-start(bf16[1,1000,768]{2,1,0:T(8,128)(2,1)} %param.11) | copy-start | bytes 4608004
  71.0 21.6 %copy-start.1 = (bf16[1,64,768]{2,1,0:T(8,128)(2,1)S(1)}, bf16[1,64,768]{2,1,0:T(8,128)(2,1)}, u32[]{:S(2)}) copy-start(bf16[1,64,768]{2,1,0:T(8,128)(2,1)} %hidden_ref) | copy-start | bytes 294916
  71.0 21.6 %copy-start.3 = (s32[1,3]{1,0:T(1,128)S(1)}, s32[1,3]{1,0:T(1,128)}, u32[]{:S(2)}) copy-start(s32[1,3]{1,0:T(1,128)} %steps_ref.1) | copy-start | bytes 40

commit v4 on v3

v4 whole, which is shorter than its diff:
```python
import functools

import jax
import jax.numpy as jnp
from jax import lax
from jax.experimental import pallas as pl
from jax.experimental.pallas import tpu as pltpu
from jax.sharding import Mesh, PartitionSpec as P

HEAD_DIM = 128
SCALE = HEAD_DIM**-0.5 * 1.4426950408889634
MASKED = -(2.0**100)
STATS = 16
SPLIT = 2
COLUMNS = ("yl", "x")


def sample_of(positions, bound_a, bound_b):
    return (positions >= bound_a).astype(jnp.int32) + (positions >= bound_b).astype(jnp.int32)


def bounds(lengths_ref, tower):
    first = lengths_ref[tower, 0, 0]
    return first, first + lengths_ref[tower, 0, 1]


def position(yh, yl, x, zhi, row, rows):
    column = (yl * lax.axis_size("yh") + yh) * lax.axis_size("x") + x
    return (column * lax.axis_size("zhi") + zhi) * rows + row


def pack_kernel(steps_ref, q_ref, k_ref, v_ref, table_ref, out_ref, gates_ref, found, sems):
    fetches = [
        pltpu.make_async_copy(table_ref.at[steps_ref[0, i] // 8], found.at[i], sems.at[i])
        for i in range(3)
    ]
    for fetch in fetches:
        fetch.start()
    pairs, triple, width = out_ref.shape
    halves = lax.axis_size("yh")
    groups, rows = pairs // halves, triple // 3
    for i, ref in enumerate((q_ref, k_ref, v_ref)):
        for s in range(halves):
            for g in range(groups):
                cols = slice((g * halves + s) * width, (g * halves + s + 1) * width)
                out_ref[s * groups + g, i * rows : (i + 1) * rows] = ref[0, :, cols]
    gates_ref[...] = jnp.zeros(gates_ref.shape, jnp.float32)
    for i, fetch in enumerate(fetches):
        fetch.wait()
        wanted = lax.broadcasted_iota(jnp.int32, (8, 1), 0) == steps_ref[0, i] % 8
        row = jnp.where(wanted, found[i].astype(jnp.float32), 0.0)
        gates_ref[i : i + 1] = jnp.sum(row, axis=0, keepdims=True)


def copies_kernel(in_ref, q_ref, kv_ref):
    sources, triple, _ = in_ref.shape[1:]
    rows = triple // 3
    mine = lax.axis_index("tower")
    other = 1 - mine
    for g in range(sources):
        q = in_ref[mine, g, :rows]
        for c in range(q_ref.shape[0]):
            q_ref[c, g * rows : (g + 1) * rows] = q
        k = in_ref[other, g, rows : 2 * rows]
        v = in_ref[other, g, 2 * rows :]
        for c in range(kv_ref.shape[0]):
            kv_ref[c, g * rows : (g + 1) * rows] = k
            kv_ref[c, (sources + g) * rows : (sources + g + 1) * rows] = v


def place(over_z, i, within, rows):
    if over_z:
        yl, x, zhi = lax.axis_index("yl"), lax.axis_index("x"), i
    else:
        yl, x, zhi = i // lax.axis_size("x"), i % lax.axis_size("x"), lax.axis_index("zhi")
    return position(within // rows, yl, x, zhi, within % rows, rows)


def attend_kernel(keys_over_z, lengths_ref, q_ref, kv_ref, out_ref):
    blocks, part, width = q_ref.shape
    heads = width // HEAD_DIM
    halves = lax.axis_size("yh")
    rows = part // halves
    keys = kv_ref.shape[0] * part
    tile = blocks * part
    tower = lax.axis_index("tower")
    own_a, own_b = bounds(lengths_ref, tower)
    far_a, far_b = bounds(lengths_ref, 1 - tower)

    lane = lax.broadcasted_iota(jnp.int32, (1, keys), 1)
    key_ids = sample_of(place(keys_over_z, lane // part, lane % part, rows), far_a, far_b)
    r = lax.broadcasted_iota(jnp.int32, (tile, 1), 0)
    query_at = place(not keys_over_z, r // part, r % part, rows)
    lane = lax.broadcasted_iota(jnp.int32, (1, HEAD_DIM), 1)
    allowed = sample_of(query_at, own_a, own_b) == key_ids
    stats = jnp.zeros((tile, HEAD_DIM), jnp.float32)
    for h in range(heads):
        cols = slice(h * HEAD_DIM, (h + 1) * HEAD_DIM)
        q = q_ref[:, :, cols].reshape(tile, HEAD_DIM)
        k = kv_ref[:, :part, cols].reshape(keys, HEAD_DIM)
        v = kv_ref[:, part:, cols].reshape(keys, HEAD_DIM)
        s = lax.dot_general(q, k, (((1,), (1,)), ((), ())), preferred_element_type=jnp.float32)
        s = jnp.where(allowed, s, MASKED)
        top = (jnp.max(s, axis=1, keepdims=True) * SCALE).astype(jnp.bfloat16)
        top = top.astype(jnp.float32)
        empty = top < 0.01 * MASKED
        shift = jnp.where(empty, 0.0, top)
        p = jnp.exp2(s * SCALE - shift)
        total = jnp.sum(p, axis=1, keepdims=True)
        o = jnp.dot(p.astype(jnp.bfloat16), v, preferred_element_type=jnp.float32)
        high = total.astype(jnp.bfloat16).astype(jnp.float32)
        stats = jnp.where(lane == h, jnp.where(empty, MASKED, top), stats)
        stats = jnp.where(lane == 4 + h, total - high, stats)
        stats = jnp.where(lane == 8 + h, high, stats)
        o = o.astype(jnp.bfloat16).reshape(blocks, halves, rows, HEAD_DIM)
        for s2 in range(halves):
            out_ref[s2, :, h * rows : (h + 1) * rows, :] = o[:, s2]
    pick = lax.broadcasted_iota(jnp.int32, (STATS, 1), 0) == lane
    stats = lax.dot_general(
        jnp.where(pick, 1.0, 0.0).astype(jnp.bfloat16),
        stats.astype(jnp.bfloat16),
        (((1,), (1,)), ((), ())),
        preferred_element_type=jnp.float32,
    ).astype(jnp.bfloat16)
    for c in range(blocks):
        for s2 in range(halves):
            at = (c * halves + s2) * rows
            out_ref[s2, c, heads * rows :, :rows] = stats[:, at : at + rows]
            out_ref[s2, c, heads * rows :, rows:] = jnp.zeros(
                (STATS, HEAD_DIM - rows), jnp.bfloat16
            )


def merge_kernel(lengths_ref, parts_ref, hidden_ref, gates_ref, out_ref):
    halves, columns, full, _ = parts_ref.shape
    rows = hidden_ref.shape[1]
    heads = (full - STATS) // rows
    own_a, own_b = bounds(lengths_ref, lax.axis_index("tower"))
    yh, yl, x = lax.axis_index("yh"), lax.axis_index("yl"), lax.axis_index("x")
    row = lax.broadcasted_iota(jnp.int32, (rows, 1), 0)
    ids = sample_of(position(yh, yl, x, lax.axis_index("zhi"), row, rows), own_a, own_b)

    scales = []
    for s2 in range(halves):
        stats = [parts_ref[s2, j, heads * rows :, :].astype(jnp.float32) for j in range(columns)]
        tops = [st[:8] for st in stats]
        top = functools.reduce(jnp.maximum, tops)
        factors, total = [], jnp.zeros_like(top)
        for st in stats:
            factor = jnp.exp2(jnp.minimum(st[:8] - top, 0.0))
            sums = st[8:] + jnp.concatenate([st[4:8], st[:4]], axis=0)
            factors.append(factor)
            total = total + factor * sums
        inverse = 1.0 / jnp.where(total > 0.0, total, 1.0)
        scales += [factor * inverse for factor in factors]
    scales = jnp.concatenate(scales, axis=0).T
    for s2 in range(halves):
        for h in range(heads):
            o = jnp.zeros((rows, HEAD_DIM), jnp.float32)
            for j in range(columns):
                part = parts_ref[s2, j, h * rows : (h + 1) * rows, :].astype(jnp.float32)
                at = (s2 * columns + j) * 8 + h
                o = o + scales[:rows, at : at + 1] * part
            cols = slice((s2 * heads + h) * HEAD_DIM, (s2 * heads + h + 1) * HEAD_DIM)
            gate = jnp.where(
                ids == 0,
                gates_ref[0:1, cols],
                jnp.where(ids == 1, gates_ref[1:2, cols], gates_ref[2:3, cols]),
            )
            out_ref[0, :, cols] = (hidden_ref[0, :, cols].astype(jnp.float32) + gate * o).astype(
                jnp.bfloat16
            )


def vmem(n):
    return [pl.BlockSpec(memory_space=pltpu.VMEM)] * n


SMEM = pl.BlockSpec(memory_space=pltpu.SMEM)
HBM = pl.BlockSpec(memory_space=pltpu.HBM)


def params(mib):
    return pltpu.CompilerParams(vmem_limit_bytes=mib * 1024 * 1024)


def shards(queries, key_rows, value_rows, hidden, gate_table, lengths, step_ids):
    groups = lax.axis_size("head")
    halves = lax.axis_size("yh")
    columns = lax.axis_size(COLUMNS)
    chunks = lax.axis_size("zhi")
    rows, width = queries.shape[1], queries.shape[2] // (groups * halves)
    heads = width // HEAD_DIM
    part = rows * groups * halves

    table = gate_table.reshape(gate_table.shape[1] // 8, 8, gate_table.shape[2])
    sent, gates = pl.pallas_call(
        pack_kernel,
        out_shape=(
            jax.ShapeDtypeStruct((halves * groups, 3 * rows, width), jnp.bfloat16),
            jax.ShapeDtypeStruct((8, table.shape[2]), jnp.float32),
        ),
        in_specs=[SMEM] + vmem(3) + [HBM],
        out_specs=tuple(vmem(2)),
        scratch_shapes=[
            pltpu.VMEM((3,) + table.shape[1:], jnp.bfloat16),
            pltpu.SemaphoreType.DMA((3,)),
        ],
        compiler_params=params(60),
        name="pack",
    )(step_ids, queries, key_rows, value_rows, table)
    sent = lax.all_to_all(sent, ("yh", "head"), 0, 0, tiled=True)
    sent = lax.all_gather(sent, "tower", axis=0, tiled=False)
    def finish(keys_over_z, back, qs, kv, hidden, gates):
        shape = (halves, qs.shape[0], heads * (part // halves) + STATS, HEAD_DIM)
        parts = pl.pallas_call(
            functools.partial(attend_kernel, keys_over_z),
            out_shape=jax.ShapeDtypeStruct(shape, jnp.bfloat16),
            in_specs=[SMEM] + vmem(2),
            out_specs=vmem(1)[0],
            compiler_params=params(24),
            name="attend",
        )(lengths, qs, kv)
        parts, hidden, gates = lax.optimization_barrier((parts, hidden, gates))
        parts = lax.all_to_all(
            parts.reshape((shape[0] * shape[1],) + shape[2:]), ("yh",) + back, 0, 0, tiled=True
        )
        return pl.pallas_call(
            merge_kernel,
            out_shape=jax.ShapeDtypeStruct(hidden.shape, jnp.bfloat16),
            in_specs=[SMEM] + vmem(3),
            out_specs=vmem(1)[0],
            compiler_params=params(16),
            name="merge",
        )(lengths, parts.reshape(shape), hidden, gates)

    def split(sent, query_copies, key_copies):
        return pl.pallas_call(
            copies_kernel,
            out_shape=(
                jax.ShapeDtypeStruct((query_copies, part, width), jnp.bfloat16),
                jax.ShapeDtypeStruct((key_copies, 2 * part, width), jnp.bfloat16),
            ),
            in_specs=vmem(1),
            out_specs=tuple(vmem(2)),
            compiler_params=params(8),
            name="copies",
        )(sent)

    def keys_beside(sent, hidden, gates):
        qs, kv = split(sent, columns, 1)
        qs = lax.all_to_all(qs, COLUMNS, 0, 0, tiled=True)
        kv = lax.all_gather(kv[0], "zhi", axis=0, tiled=True).reshape(chunks, 2 * part, width)
        return finish(True, COLUMNS, qs, kv, hidden, gates)

    def keys_first(sent, hidden, gates):
        qs, kv = split(sent, columns, 1)
        kv = lax.all_gather(kv[0], "zhi", axis=0, tiled=True).reshape(chunks, 2 * part, width)
        qs, kv = lax.optimization_barrier((qs, kv))
        qs = lax.all_to_all(qs, COLUMNS, 0, 0, tiled=True)
        return finish(True, COLUMNS, qs, kv, hidden, gates)

    def queries_beside(sent, hidden, gates):
        qs, kv = split(sent, 1, columns)
        kv = lax.all_to_all(kv, COLUMNS, 0, 0, tiled=True)
        qs = lax.all_gather(qs[0], "zhi", axis=0, tiled=True).reshape(chunks, part, width)
        return finish(False, ("zhi",), qs, kv, hidden, gates)

    plane = lax.axis_index("head")
    which = ((plane == 0) + 2 * (plane == 2) + 2 * (plane == 3)).astype(jnp.int32)
    return lax.switch(which, [keys_first, keys_beside, queries_beside], sent, hidden, gates)


def solution(mesh):
    towers, seq, head = mesh.devices.shape
    fine = Mesh(
        mesh.devices.reshape(towers, 4 // SPLIT, SPLIT, 4, seq // 16, head),
        ("tower", "yl", "yh", "x", "zhi", "head"),
    )
    seq_axes = ("yl", "yh", "x", "zhi")
    rows = P("tower", seq_axes + ("head",), None)
    block = P("tower", seq_axes, "head")
    return jax.shard_map(
        shards,
        mesh=fine,
        in_specs=(rows, rows, rows, block, P("tower", None, "head"), P(), P()),
        out_specs=block,
        check_vma=False,
    )
```

time: 94.8 us -> 87.6 us (0.924)
  the two profiles are of different devices: /device:TPU:2 before, /device:TPU:1 now
where the time goes in v4:
time: 87.6 us; the launch traced here: 86.7 us
  blocking collectives  55.9 us (64%)
  starting transfers between devices  13.6 us (16%)
  Pallas kernels  8.4 us (10%)
  waiting for transfers between devices  7.8 us (9%)
    all_gather x1, blocking collectives, keys_beside(): lax.all_gather(kv[0], 'zhi', axis=0, tiled=True)  30.3 us
    all_to_all x1, blocking collectives, finish(): lax.all_to_all(parts.reshape((shape[0] * shape[1],) + shape[2:]), ('yh',)...  20 us
    all_to_all x1, waiting for transfers between devices, shards(): sent = lax.all_to_all(sent, ('yh', 'head'), 0, 0, tiled=True)  7.79 us
    all_to_all x1, starting transfers between devices, shards(): sent = lax.all_to_all(sent, ('yh', 'head'), 0, 0, tiled=True)  7.48 us
    all_to_all x1, starting transfers between devices, keys_beside(): qs = lax.all_to_all(qs, COLUMNS, 0, 0, tiled=True)  6.17 us
    all_gather x1, blocking collectives, shards(): sent = lax.all_gather(sent, 'tower', axis=0, tiled=False)  5.67 us
    pallas_call x1, Pallas kernels, finish(): pl.pallas_call(functools.partial(attend_kernel, keys_over_z), out_shape=j...  3.63 us
    pallas_call x1, Pallas kernels, shards(): pl.pallas_call(pack_kernel, out_shape=(jax.ShapeDtypeStruct((halves * gro...  2.53 us
  transfers between devices with their start and end apart: 2, of which 1 were waited for; matrix products, arithmetic and copies ran while one was open for 0% of the time, Pallas kernels for 0%

profile of v4, /device:TPU:1, one launch (start us, length us, event | category | flops | bytes accessed | tf_op | source)
XLA Modules:
  0.0 86.7 jit_solution(15236445690879262747)
XLA Ops:
  0.0 0.0 copy-start
  0.0 0.0 copy-start.2
  0.0 2.5 %pack.1 = (bf16[8,48,384]{2,1,0:T(8,128)(2,1)}, f32[8,768]{1,0:T(8,128)S(1)}) custom-call(s32[1,3]{1,0:T(1,128)} %steps_ref.1, bf16[1,16,3072]{2,1,0:T(8,128)(2,1)} %q_ref.1, bf16[1,16,3072]{2,1,0:T(8,128)(2,1)} %k_ref.1, bf16[1,16,3072]{2,1,0:T(8,128)(2,1)} %v_ref.1, bf16[125,8,768]{2,1,0:T(8,128)(2,1)} %bitcast.23), custom_call_target="tpu_custom_call" | custom-call | tf_op jit(solution)/shard_map/pack/pallas_call | solution.py:197
  2.5 7.5 %all-to-all-start.6 = ((bf16[8,48,384]{2,1,0:T(8,128)(2,1)}), bf16[8,48,384]{2,1,0:T(8,128)(2,1)S(1)}, u32[]{:S(2)}, u32[]{:S(2)}) async-start(bf16[8,48,384]{2,1,0:T(8,128)(2,1)} %get-tuple-element.64), calls=%async_computation.6 | async-start | bytes 589824 | tf_op jit(solution)/shard_map/all_to_all | solution.py:212
  10.0 7.8 %all-to-all-done.6 = bf16[8,48,384]{2,1,0:T(8,128)(2,1)S(1)} async-done(((bf16[8,48,384]{2,1,0:T(8,128)(2,1)}), bf16[8,48,384]{2,1,0:T(8,128)(2,1)S(1)}, u32[]{:S(2)}, u32[]{:S(2)}) %all-to-all-start.6) | async-done | bytes 294944 | tf_op jit(solution)/shard_map/all_to_all | solution.py:212
  17.8 5.7 %all-gather.3 = bf16[16,48,384]{2,1,0:T(8,128)(2,1)S(1)} all-gather(bf16[8,48,384]{2,1,0:T(8,128)(2,1)S(1)} %all-to-all-done.6), channel_id=5, replica_groups=mesh['tower'=2,'yl'=2,'yh'=2,'x'=4,'zhi'=4,'head'=4] {'tower'}, dimensions={0}, use_global_device_ids=true | all-gather | bytes 884736 | tf_op jit(solution)/shard_map/all_gather | solution.py:213
  23.5 0.0 copy-done
  23.5 0.0 copy-done.2
  23.5 62.6 %conditional.1 = (bf16[1,64,768]{2,1,0:T(8,128)(2,1)S(1)}) conditional(s32[]{:T(128)} %clamp.3, (bf16[2,8,48,384]{3,2,1,0:T(8,128)(2,1)S(1)}, s32[2,1,3]{2,1,0:T(1,128)S(1)}, bf16[1,64,768]{2,1,0:T(8,128)(2,1)S(1)}, f32[8,768]{1,0:T(8,128)S(1)}) %tuple.32, (bf16[2,8,48,384]{3,2,1,0:T(8,128)(2,1)S(1)}, s32[2,1,3]{2,1,0:T(1,128)S(1)}, ...), branch_computations={%region_0.0_spmd, %region_1.0_spmd, %region_2.0_spmd} | conditional | bytes 6062120 | solution.py:271
  23.5 1.0 %copies.4 = (bf16[8,128,384]{2,1,0:T(8,128)(2,1)}, bf16[1,256,384]{2,1,0:T(8,128)(2,1)S(1)}) custom-call(bf16[2,8,48,384]{3,2,1,0:T(8,128)(2,1)S(1)} %get-tuple-element.45.in_ref), custom_call_target="tpu_custom_call" | custom-call | tf_op jit(solution)/shard_map/cond/branch_1_fun/copies/pallas_call | solution.py:238
  24.5 6.2 %all-to-all-start.2 = ((bf16[8,128,384]{2,1,0:T(8,128)(2,1)}), bf16[8,128,384]{2,1,0:T(8,128)(2,1)S(1)}, u32[]{:S(2)}, u32[]{:S(2)}) async-start(bf16[8,128,384]{2,1,0:T(8,128)(2,1)} %get-tuple-element.46), calls=%async_computation.2 | async-start | bytes 1572864 | tf_op jit(solution)/shard_map/cond/branch_1_fun/all_to_all | solution.py:252
  30.6 30.3 %all-gather.1 = bf16[1,1024,384]{2,1,0:T(8,128)(2,1)S(1)} all-gather(bf16[1,256,384]{2,1,0:T(8,128)(2,1)S(1)} %get-tuple-element.47), channel_id=3, replica_groups=mesh['tower'=2,'yl'=2,'yh'=2,'x'=4,'zhi'=4,'head'=4] {'zhi'}, dimensions={1}, use_global_device_ids=true | all-gather | bytes 983040 | tf_op jit(solution)/shard_map/cond/branch_1_fun/all_gather | solution.py:253
  60.9 0.0 all-to-all-done.2.q_ref
  60.9 3.6 %attend.4 = bf16[2,8,208,128]{3,2,1,0:T(8,128)(2,1)S(1)} custom-call(s32[2,1,3]{2,1,0:T(1,128)S(1)} %get-tuple-element.74.lengths_ref, bf16[8,128,384]{2,1,0:T(8,128)(2,1)S(1)} %all-to-all-done.2.q_ref, bf16[4,256,384]{2,1,0:T(8,128)(2,1)S(1)} %bitcast.15), custom_call_target="tpu_custom_call" | custom-call | tf_op jit(solution)/shard_map/cond/branch_1_fun/attend/pallas_call | solution.py:216
  64.5 20.0 %all_to_all.31 = bf16[16,208,128]{2,1,0:T(8,128)(2,1)S(1)} all-to-all(bf16[16,208,128]{2,1,0:T(8,128)(2,1)S(1)} %bitcast.14), channel_id=1, replica_groups=mesh['tower'=2,'yl'=2,'yh'=2,'x'=4,'zhi'=4,'head'=4] {'yh','yl','x'}, dimensions={0} | all-to-all | bytes 1703936 | tf_op jit(solution)/shard_map/cond/branch_1_fun/all_to_all | solution.py:225
  84.6 1.3 %merge.4 = bf16[1,64,768]{2,1,0:T(8,128)(2,1)S(1)} custom-call(s32[2,1,3]{2,1,0:T(1,128)S(1)} %get-tuple-element.74.lengths_ref, bf16[2,8,208,128]{3,2,1,0:T(8,128)(2,1)S(1)} %bitcast.12, bf16[1,64,768]{2,1,0:T(8,128)(2,1)S(1)} %get-tuple-element.51.hidden_ref, f32[8,768]{1,0:T(8,128)S(1)} %get-tuple-element.52.gates_ref), custom_call_target="tpu_custom_call" | custom-call | tf_op jit(solution)/shard_map/cond/branch_1_fun/merge/pallas_call | solution.py:228
  86.0 0.0 copy-start.1
  86.1 0.6 copy-done.1
Async XLA Ops:
  0.0 23.5 %copy-start = (bf16[1,64,768]{2,1,0:T(8,128)(2,1)S(1)}, bf16[1,64,768]{2,1,0:T(8,128)(2,1)}, u32[]{:S(2)}) copy-start(bf16[1,64,768]{2,1,0:T(8,128)(2,1)} %param.13) | copy-start | bytes 294916
  0.0 23.5 %copy-start.2 = (s32[2,1,3]{2,1,0:T(1,128)S(1)}, s32[2,1,3]{2,1,0:T(1,128)}, u32[]{:S(2)}) copy-start(s32[2,1,3]{2,1,0:T(1,128)} %param.15) | copy-start | bytes 76
  2.5 15.3 %all-to-all-start.6 = ((bf16[8,48,384]{2,1,0:T(8,128)(2,1)}), bf16[8,48,384]{2,1,0:T(8,128)(2,1)S(1)}, u32[]{:S(2)}, u32[]{:S(2)}) async-start(bf16[8,48,384]{2,1,0:T(8,128)(2,1)} %get-tuple-element.64), calls=%async_computation.6 | async-start | bytes 589824 | tf_op jit(solution)/shard_map/all_to_all | solution.py:212
  24.5 36.4 %all-to-all-start.2 = ((bf16[8,128,384]{2,1,0:T(8,128)(2,1)}), bf16[8,128,384]{2,1,0:T(8,128)(2,1)S(1)}, u32[]{:S(2)}, u32[]{:S(2)}) async-start(bf16[8,128,384]{2,1,0:T(8,128)(2,1)} %get-tuple-element.46), calls=%async_computation.2 | async-start | bytes 1572864 | tf_op jit(solution)/shard_map/cond/branch_1_fun/all_to_all | solution.py:252
  86.0 0.6 copy-start.1

commit v5 on v4

--- a/solution.py
+++ b/solution.py
@@ -29,13 +29,7 @@
     return (column * lax.axis_size("zhi") + zhi) * rows + row
 
 
-def pack_kernel(steps_ref, q_ref, k_ref, v_ref, table_ref, out_ref, gates_ref, found, sems):
-    fetches = [
-        pltpu.make_async_copy(table_ref.at[steps_ref[0, i] // 8], found.at[i], sems.at[i])
-        for i in range(3)
-    ]
-    for fetch in fetches:
-        fetch.start()
+def pack_kernel(q_ref, k_ref, v_ref, out_ref):
     pairs, triple, width = out_ref.shape
     halves = lax.axis_size("yh")
     groups, rows = pairs // halves, triple // 3
@@ -44,6 +38,15 @@
             for g in range(groups):
                 cols = slice((g * halves + s) * width, (g * halves + s + 1) * width)
                 out_ref[s * groups + g, i * rows : (i + 1) * rows] = ref[0, :, cols]
+
+
+def gates_kernel(steps_ref, table_ref, gates_ref, found, sems):
+    fetches = [
+        pltpu.make_async_copy(table_ref.at[steps_ref[0, i] // 8], found.at[i], sems.at[i])
+        for i in range(3)
+    ]
+    for fetch in fetches:
+        fetch.start()
     gates_ref[...] = jnp.zeros(gates_ref.shape, jnp.float32)
     for i, fetch in enumerate(fetches):
         fetch.wait()
@@ -193,22 +196,28 @@
     heads = width // HEAD_DIM
     part = rows * groups * halves
 
+    sent = pl.pallas_call(
+        pack_kernel,
+        out_shape=jax.ShapeDtypeStruct((halves * groups, 3 * rows, width), jnp.bfloat16),
+        in_specs=vmem(3),
+        out_specs=vmem(1)[0],
+        compiler_params=params(60),
+        name="pack",
+    )(queries, key_rows, value_rows)
     table = gate_table.reshape(gate_table.shape[1] // 8, 8, gate_table.shape[2])
-    sent, gates = pl.pallas_call(
-        pack_kernel,
-        out_shape=(
-            jax.ShapeDtypeStruct((halves * groups, 3 * rows, width), jnp.bfloat16),
-            jax.ShapeDtypeStruct((8, table.shape[2]), jnp.float32),
-        ),
-        in_specs=[SMEM] + vmem(3) + [HBM],
-        out_specs=tuple(vmem(2)),
+    gates = pl.pallas_call(
+        gates_kernel,
+        out_shape=jax.ShapeDtypeStruct((8, table.shape[2]), jnp.float32),
+        in_specs=[SMEM, HBM],
+        out_specs=vmem(1)[0],
         scratch_shapes=[
             pltpu.VMEM((3,) + table.shape[1:], jnp.bfloat16),
             pltpu.SemaphoreType.DMA((3,)),
         ],
         compiler_params=params(60),
-        name="pack",
-    )(step_ids, queries, key_rows, value_rows, table)
+        cost_estimate=pl.CostEstimate(flops=100000, bytes_accessed=100000, transcendentals=0),
+        name="gates",
+    )(step_ids, table)
     sent = lax.all_to_all(sent, ("yh", "head"), 0, 0, tiled=True)
     sent = lax.all_gather(sent, "tower", axis=0, tiled=False)
     def finish(keys_over_z, back, qs, kv, hidden, gates):

time: 87.6 us -> 86.7 us (0.990)
  waiting for transfers between devices: 7.8 us -> 6.31 us
    all_to_all x1, waiting for transfers between devices: 7.79 us -> 6.31 us  [shards(): sent = lax.all_to_all(sent, ('yh', 'head'), 0, 0, tiled=True)]
    pallas_call x1 -> x2, Pallas kernels: 2.53 us -> 3.17 us  [the longest x1 1.71 us: shards(): pl.pallas_call(pack_kernel, out_shape=jax.ShapeDtypeStruct((halves * grou...]
  transfers between devices with their start and end apart: 2 -> 2, of which waited for: 1 -> 1; matrix products, arithmetic and copies ran while one was open for 0% -> 0% of each run, Pallas kernels for 0% -> 2%
where the time goes in v5:
time: 86.7 us; the launch traced here: 85.9 us
  blocking collectives  55.8 us (64%)
  starting transfers between devices  13.8 us (16%)
  Pallas kernels  9.04 us (10%)
  waiting for transfers between devices  6.31 us (7%)
    all_gather x1, blocking collectives, keys_beside(): lax.all_gather(kv[0], 'zhi', axis=0, tiled=True)  29.7 us
    all_to_all x1, blocking collectives, finish(): lax.all_to_all(parts.reshape((shape[0] * shape[1],) + shape[2:]), ('yh',)...  20.5 us
    all_to_all x1, starting transfers between devices, shards(): sent = lax.all_to_all(sent, ('yh', 'head'), 0, 0, tiled=True)  7.59 us
    all_to_all x1, waiting for transfers between devices, shards(): sent = lax.all_to_all(sent, ('yh', 'head'), 0, 0, tiled=True)  6.31 us
    all_to_all x1, starting transfers between devices, keys_beside(): qs = lax.all_to_all(qs, COLUMNS, 0, 0, tiled=True)  6.17 us
    all_gather x1, blocking collectives, shards(): sent = lax.all_gather(sent, 'tower', axis=0, tiled=False)  5.67 us
    pallas_call x1, Pallas kernels, finish(): pl.pallas_call(functools.partial(attend_kernel, keys_over_z), out_shape=j...  3.63 us
  transfers between devices with their start and end apart: 2, of which 1 were waited for; matrix products, arithmetic and copies ran while one was open for 0% of the time, Pallas kernels for 2%

profile of v5, /device:TPU:1, one launch (start us, length us, event | category | flops | bytes accessed | tf_op | source)
XLA Modules:
  0.0 85.9 jit_solution(7456398857493353221)
XLA Ops:
  0.0 1.7 %pack.1 = bf16[8,48,384]{2,1,0:T(8,128)(2,1)} custom-call(bf16[1,16,3072]{2,1,0:T(8,128)(2,1)} %q_ref.1, bf16[1,16,3072]{2,1,0:T(8,128)(2,1)} %k_ref.1, bf16[1,16,3072]{2,1,0:T(8,128)(2,1)} %v_ref.1), custom_call_target="tpu_custom_call" | custom-call | tf_op jit(solution)/shard_map/pack/pallas_call | solution.py:199
  1.7 0.0 copy-start
  1.7 0.0 copy-start.2
  1.7 7.6 %all-to-all-start.6 = ((bf16[8,48,384]{2,1,0:T(8,128)(2,1)}), bf16[8,48,384]{2,1,0:T(8,128)(2,1)S(1)}, u32[]{:S(2)}, u32[]{:S(2)}) async-start(bf16[8,48,384]{2,1,0:T(8,128)(2,1)} %pack.1), calls=%async_computation.6 | async-start | bytes 589824 | tf_op jit(solution)/shard_map/all_to_all | solution.py:221
  9.3 1.5 %gates.1 = f32[8,768]{1,0:T(8,128)S(1)} custom-call(s32[1,3]{1,0:T(1,128)} %steps_ref.1, bf16[125,8,768]{2,1,0:T(8,128)(2,1)} %bitcast.23), custom_call_target="tpu_custom_call" | custom-call | flops 100000 | bytes 100000 | tf_op jit(solution)/shard_map/gates/pallas_call | solution.py:208
  10.8 6.3 %all-to-all-done.6 = bf16[8,48,384]{2,1,0:T(8,128)(2,1)S(1)} async-done(((bf16[8,48,384]{2,1,0:T(8,128)(2,1)}), bf16[8,48,384]{2,1,0:T(8,128)(2,1)S(1)}, u32[]{:S(2)}, u32[]{:S(2)}) %all-to-all-start.6) | async-done | bytes 294944 | tf_op jit(solution)/shard_map/all_to_all | solution.py:221
  17.1 5.7 %all-gather.3 = bf16[16,48,384]{2,1,0:T(8,128)(2,1)S(1)} all-gather(bf16[8,48,384]{2,1,0:T(8,128)(2,1)S(1)} %all-to-all-done.6), channel_id=5, replica_groups=mesh['tower'=2,'yl'=2,'yh'=2,'x'=4,'zhi'=4,'head'=4] {'tower'}, dimensions={0}, use_global_device_ids=true | all-gather | bytes 884736 | tf_op jit(solution)/shard_map/all_gather | solution.py:222
  22.8 0.0 copy-done
  22.8 0.0 copy-done.2
  22.8 62.4 %conditional.1 = (bf16[1,64,768]{2,1,0:T(8,128)(2,1)S(1)}) conditional(s32[]{:T(128)} %clamp.3, (bf16[2,8,48,384]{3,2,1,0:T(8,128)(2,1)S(1)}, s32[2,1,3]{2,1,0:T(1,128)S(1)}, bf16[1,64,768]{2,1,0:T(8,128)(2,1)S(1)}, f32[8,768]{1,0:T(8,128)S(1)}) %tuple.32, (bf16[2,8,48,384]{3,2,1,0:T(8,128)(2,1)S(1)}, s32[2,1,3]{2,1,0:T(1,128)S(1)}, ...), branch_computations={%region_0.0_spmd, %region_1.0_spmd, %region_2.0_spmd} | conditional | bytes 6062120 | solution.py:280
  22.8 1.0 %copies.4 = (bf16[8,128,384]{2,1,0:T(8,128)(2,1)}, bf16[1,256,384]{2,1,0:T(8,128)(2,1)S(1)}) custom-call(bf16[2,8,48,384]{3,2,1,0:T(8,128)(2,1)S(1)} %get-tuple-element.45.in_ref), custom_call_target="tpu_custom_call" | custom-call | tf_op jit(solution)/shard_map/cond/branch_1_fun/copies/pallas_call | solution.py:247
  23.8 6.2 %all-to-all-start.2 = ((bf16[8,128,384]{2,1,0:T(8,128)(2,1)}), bf16[8,128,384]{2,1,0:T(8,128)(2,1)S(1)}, u32[]{:S(2)}, u32[]{:S(2)}) async-start(bf16[8,128,384]{2,1,0:T(8,128)(2,1)} %get-tuple-element.46), calls=%async_computation.2 | async-start | bytes 1572864 | tf_op jit(solution)/shard_map/cond/branch_1_fun/all_to_all | solution.py:261
  29.9 29.7 %all-gather.1 = bf16[1,1024,384]{2,1,0:T(8,128)(2,1)S(1)} all-gather(bf16[1,256,384]{2,1,0:T(8,128)(2,1)S(1)} %get-tuple-element.47), channel_id=3, replica_groups=mesh['tower'=2,'yl'=2,'yh'=2,'x'=4,'zhi'=4,'head'=4] {'zhi'}, dimensions={1}, use_global_device_ids=true | all-gather | bytes 983040 | tf_op jit(solution)/shard_map/cond/branch_1_fun/all_gather | solution.py:262
  59.6 0.0 all-to-all-done.2.q_ref
  59.6 3.6 %attend.4 = bf16[2,8,208,128]{3,2,1,0:T(8,128)(2,1)S(1)} custom-call(s32[2,1,3]{2,1,0:T(1,128)S(1)} %get-tuple-element.70.lengths_ref, bf16[8,128,384]{2,1,0:T(8,128)(2,1)S(1)} %all-to-all-done.2.q_ref, bf16[4,256,384]{2,1,0:T(8,128)(2,1)S(1)} %bitcast.15), custom_call_target="tpu_custom_call" | custom-call | tf_op jit(solution)/shard_map/cond/branch_1_fun/attend/pallas_call | solution.py:225
  63.2 20.5 %all_to_all.31 = bf16[16,208,128]{2,1,0:T(8,128)(2,1)S(1)} all-to-all(bf16[16,208,128]{2,1,0:T(8,128)(2,1)S(1)} %bitcast.14), channel_id=1, replica_groups=mesh['tower'=2,'yl'=2,'yh'=2,'x'=4,'zhi'=4,'head'=4] {'yh','yl','x'}, dimensions={0} | all-to-all | bytes 1703936 | tf_op jit(solution)/shard_map/cond/branch_1_fun/all_to_all | solution.py:234
  83.7 1.3 %merge.4 = bf16[1,64,768]{2,1,0:T(8,128)(2,1)S(1)} custom-call(s32[2,1,3]{2,1,0:T(1,128)S(1)} %get-tuple-element.70.lengths_ref, bf16[2,8,208,128]{3,2,1,0:T(8,128)(2,1)S(1)} %bitcast.12, bf16[1,64,768]{2,1,0:T(8,128)(2,1)S(1)} %get-tuple-element.51.hidden_ref, f32[8,768]{1,0:T(8,128)S(1)} %get-tuple-element.52.gates_ref), custom_call_target="tpu_custom_call" | custom-call | tf_op jit(solution)/shard_map/cond/branch_1_fun/merge/pallas_call | solution.py:237
  85.2 0.0 copy-start.1
  85.2 0.6 copy-done.1
Async XLA Ops:
  1.7 21.1 %copy-start = (bf16[1,64,768]{2,1,0:T(8,128)(2,1)S(1)}, bf16[1,64,768]{2,1,0:T(8,128)(2,1)}, u32[]{:S(2)}) copy-start(bf16[1,64,768]{2,1,0:T(8,128)(2,1)} %param.13) | copy-start | bytes 294916
  1.7 21.1 %copy-start.2 = (s32[2,1,3]{2,1,0:T(1,128)S(1)}, s32[2,1,3]{2,1,0:T(1,128)}, u32[]{:S(2)}) copy-start(s32[2,1,3]{2,1,0:T(1,128)} %param.15) | copy-start | bytes 76
  1.7 15.4 %all-to-all-start.6 = ((bf16[8,48,384]{2,1,0:T(8,128)(2,1)}), bf16[8,48,384]{2,1,0:T(8,128)(2,1)S(1)}, u32[]{:S(2)}, u32[]{:S(2)}) async-start(bf16[8,48,384]{2,1,0:T(8,128)(2,1)} %pack.1), calls=%async_computation.6 | async-start | bytes 589824 | tf_op jit(solution)/shard_map/all_to_all | solution.py:221
  23.8 35.8 %all-to-all-start.2 = ((bf16[8,128,384]{2,1,0:T(8,128)(2,1)}), bf16[8,128,384]{2,1,0:T(8,128)(2,1)S(1)}, u32[]{:S(2)}, u32[]{:S(2)}) async-start(bf16[8,128,384]{2,1,0:T(8,128)(2,1)} %get-tuple-element.46), calls=%async_computation.2 | async-start | bytes 1572864 | tf_op jit(solution)/shard_map/cond/branch_1_fun/all_to_all | solution.py:261
  85.2 0.6 copy-start.1

commit v6 on v5

--- a/solution.py
+++ b/solution.py
@@ -263,9 +263,10 @@
         return finish(True, COLUMNS, qs, kv, hidden, gates)
 
     def keys_first(sent, hidden, gates):
-        qs, kv = split(sent, columns, 1)
+        qs, kv = split(sent, 1, 1)
         kv = lax.all_gather(kv[0], "zhi", axis=0, tiled=True).reshape(chunks, 2 * part, width)
         qs, kv = lax.optimization_barrier((qs, kv))
+        qs = jnp.broadcast_to(qs, (columns,) + qs.shape[1:])
         qs = lax.all_to_all(qs, COLUMNS, 0, 0, tiled=True)
         return finish(True, COLUMNS, qs, kv, hidden, gates)
 

time: 86.7 us -> 86.7 us (level)
  no operation moved by 1% of the time
where the time goes in v6:
time: 86.7 us; the launch traced here: 85.7 us
  blocking collectives  55.7 us (64%)
  starting transfers between devices  13.8 us (16%)
  Pallas kernels  9.04 us (10%)
  waiting for transfers between devices  6.31 us (7%)
    all_gather x1, blocking collectives, keys_beside(): lax.all_gather(kv[0], 'zhi', axis=0, tiled=True)  29.6 us
    all_to_all x1, blocking collectives, finish(): lax.all_to_all(parts.reshape((shape[0] * shape[1],) + shape[2:]), ('yh',)...  20.4 us
    all_to_all x1, starting transfers between devices, shards(): sent = lax.all_to_all(sent, ('yh', 'head'), 0, 0, tiled=True)  7.59 us
    all_to_all x1, waiting for transfers between devices, shards(): sent = lax.all_to_all(sent, ('yh', 'head'), 0, 0, tiled=True)  6.31 us
    all_to_all x1, starting transfers between devices, keys_beside(): qs = lax.all_to_all(qs, COLUMNS, 0, 0, tiled=True)  6.17 us
    all_gather x1, blocking collectives, shards(): sent = lax.all_gather(sent, 'tower', axis=0, tiled=False)  5.67 us
    pallas_call x1, Pallas kernels, finish(): pl.pallas_call(functools.partial(attend_kernel, keys_over_z), out_shape=j...  3.63 us
  transfers between devices with their start and end apart: 2, of which 1 were waited for; matrix products, arithmetic and copies ran while one was open for 0% of the time, Pallas kernels for 2%

profile of v6, /device:TPU:1, one launch (start us, length us, event | category | flops | bytes accessed | tf_op | source)
XLA Modules:
  0.0 85.7 jit_solution(14637727868379514122)
XLA Ops:
  0.0 1.7 %pack.1 = bf16[8,48,384]{2,1,0:T(8,128)(2,1)} custom-call(bf16[1,16,3072]{2,1,0:T(8,128)(2,1)} %q_ref.1, bf16[1,16,3072]{2,1,0:T(8,128)(2,1)} %k_ref.1, bf16[1,16,3072]{2,1,0:T(8,128)(2,1)} %v_ref.1), custom_call_target="tpu_custom_call" | custom-call | tf_op jit(solution)/shard_map/pack/pallas_call | solution.py:199
  1.7 0.0 copy-start
  1.7 0.0 copy-start.2
  1.7 7.6 %all-to-all-start.6 = ((bf16[8,48,384]{2,1,0:T(8,128)(2,1)}), bf16[8,48,384]{2,1,0:T(8,128)(2,1)S(1)}, u32[]{:S(2)}, u32[]{:S(2)}) async-start(bf16[8,48,384]{2,1,0:T(8,128)(2,1)} %pack.1), calls=%async_computation.6 | async-start | bytes 589824 | tf_op jit(solution)/shard_map/all_to_all | solution.py:221
  9.3 1.5 %gates.1 = f32[8,768]{1,0:T(8,128)S(1)} custom-call(s32[1,3]{1,0:T(1,128)} %steps_ref.1, bf16[125,8,768]{2,1,0:T(8,128)(2,1)} %bitcast.25), custom_call_target="tpu_custom_call" | custom-call | flops 100000 | bytes 100000 | tf_op jit(solution)/shard_map/gates/pallas_call | solution.py:208
  10.8 6.3 %all-to-all-done.6 = bf16[8,48,384]{2,1,0:T(8,128)(2,1)S(1)} async-done(((bf16[8,48,384]{2,1,0:T(8,128)(2,1)}), bf16[8,48,384]{2,1,0:T(8,128)(2,1)S(1)}, u32[]{:S(2)}, u32[]{:S(2)}) %all-to-all-start.6) | async-done | bytes 294944 | tf_op jit(solution)/shard_map/all_to_all | solution.py:221
  17.1 5.7 %all-gather.3 = bf16[16,48,384]{2,1,0:T(8,128)(2,1)S(1)} all-gather(bf16[8,48,384]{2,1,0:T(8,128)(2,1)S(1)} %all-to-all-done.6), channel_id=5, replica_groups=mesh['tower'=2,'yl'=2,'yh'=2,'x'=4,'zhi'=4,'head'=4] {'tower'}, dimensions={0}, use_global_device_ids=true | all-gather | bytes 884736 | tf_op jit(solution)/shard_map/all_gather | solution.py:222
  22.8 0.0 copy-done
  22.8 0.0 copy-done.2
  22.8 62.3 %conditional.1 = (bf16[1,64,768]{2,1,0:T(8,128)(2,1)S(1)}) conditional(s32[]{:T(128)} %clamp.3, (bf16[2,8,48,384]{3,2,1,0:T(8,128)(2,1)S(1)}, s32[2,1,3]{2,1,0:T(1,128)S(1)}, bf16[1,64,768]{2,1,0:T(8,128)(2,1)S(1)}, f32[8,768]{1,0:T(8,128)S(1)}) %tuple.32, (bf16[2,8,48,384]{3,2,1,0:T(8,128)(2,1)S(1)}, s32[2,1,3]{2,1,0:T(1,128)S(1)}, ...), branch_computations={%region_0.0_spmd, %region_1.0_spmd, %region_2.0_spmd} | conditional | bytes 6062120 | solution.py:281
  22.8 1.0 %copies.4 = (bf16[8,128,384]{2,1,0:T(8,128)(2,1)}, bf16[1,256,384]{2,1,0:T(8,128)(2,1)S(1)}) custom-call(bf16[2,8,48,384]{3,2,1,0:T(8,128)(2,1)S(1)} %get-tuple-element.45.in_ref), custom_call_target="tpu_custom_call" | custom-call | tf_op jit(solution)/shard_map/cond/branch_1_fun/copies/pallas_call | solution.py:247
  23.8 6.2 %all-to-all-start.2 = ((bf16[8,128,384]{2,1,0:T(8,128)(2,1)}), bf16[8,128,384]{2,1,0:T(8,128)(2,1)S(1)}, u32[]{:S(2)}, u32[]{:S(2)}) async-start(bf16[8,128,384]{2,1,0:T(8,128)(2,1)} %get-tuple-element.46), calls=%async_computation.2 | async-start | bytes 1572864 | tf_op jit(solution)/shard_map/cond/branch_1_fun/all_to_all | solution.py:261
  29.9 29.6 %all-gather.1 = bf16[1,1024,384]{2,1,0:T(8,128)(2,1)S(1)} all-gather(bf16[1,256,384]{2,1,0:T(8,128)(2,1)S(1)} %get-tuple-element.47), channel_id=3, replica_groups=mesh['tower'=2,'yl'=2,'yh'=2,'x'=4,'zhi'=4,'head'=4] {'zhi'}, dimensions={1}, use_global_device_ids=true | all-gather | bytes 983040 | tf_op jit(solution)/shard_map/cond/branch_1_fun/all_gather | solution.py:262
  59.5 0.0 all-to-all-done.2.q_ref
  59.5 3.6 %attend.4 = bf16[2,8,208,128]{3,2,1,0:T(8,128)(2,1)S(1)} custom-call(s32[2,1,3]{2,1,0:T(1,128)S(1)} %get-tuple-element.70.lengths_ref, bf16[8,128,384]{2,1,0:T(8,128)(2,1)S(1)} %all-to-all-done.2.q_ref, bf16[4,256,384]{2,1,0:T(8,128)(2,1)S(1)} %bitcast.16), custom_call_target="tpu_custom_call" | custom-call | tf_op jit(solution)/shard_map/cond/branch_1_fun/attend/pallas_call | solution.py:225
  63.2 20.4 %all_to_all.31 = bf16[16,208,128]{2,1,0:T(8,128)(2,1)S(1)} all-to-all(bf16[16,208,128]{2,1,0:T(8,128)(2,1)S(1)} %bitcast.15), channel_id=1, replica_groups=mesh['tower'=2,'yl'=2,'yh'=2,'x'=4,'zhi'=4,'head'=4] {'yh','yl','x'}, dimensions={0} | all-to-all | bytes 1703936 | tf_op jit(solution)/shard_map/cond/branch_1_fun/all_to_all | solution.py:234
  83.6 1.3 %merge.4 = bf16[1,64,768]{2,1,0:T(8,128)(2,1)S(1)} custom-call(s32[2,1,3]{2,1,0:T(1,128)S(1)} %get-tuple-element.70.lengths_ref, bf16[2,8,208,128]{3,2,1,0:T(8,128)(2,1)S(1)} %bitcast.13, bf16[1,64,768]{2,1,0:T(8,128)(2,1)S(1)} %get-tuple-element.51.hidden_ref, f32[8,768]{1,0:T(8,128)S(1)} %get-tuple-element.52.gates_ref), custom_call_target="tpu_custom_call" | custom-call | tf_op jit(solution)/shard_map/cond/branch_1_fun/merge/pallas_call | solution.py:237
  85.1 0.0 copy-start.1
  85.1 0.6 copy-done.1
Async XLA Ops:
  1.7 21.1 %copy-start = (bf16[1,64,768]{2,1,0:T(8,128)(2,1)S(1)}, bf16[1,64,768]{2,1,0:T(8,128)(2,1)}, u32[]{:S(2)}) copy-start(bf16[1,64,768]{2,1,0:T(8,128)(2,1)} %param.13) | copy-start | bytes 294916
  1.7 21.1 %copy-start.2 = (s32[2,1,3]{2,1,0:T(1,128)S(1)}, s32[2,1,3]{2,1,0:T(1,128)}, u32[]{:S(2)}) copy-start(s32[2,1,3]{2,1,0:T(1,128)} %param.15) | copy-start | bytes 76
  1.7 15.4 %all-to-all-start.6 = ((bf16[8,48,384]{2,1,0:T(8,128)(2,1)}), bf16[8,48,384]{2,1,0:T(8,128)(2,1)S(1)}, u32[]{:S(2)}, u32[]{:S(2)}) async-start(bf16[8,48,384]{2,1,0:T(8,128)(2,1)} %pack.1), calls=%async_computation.6 | async-start | bytes 589824 | tf_op jit(solution)/shard_map/all_to_all | solution.py:221
  23.8 35.8 %all-to-all-start.2 = ((bf16[8,128,384]{2,1,0:T(8,128)(2,1)}), bf16[8,128,384]{2,1,0:T(8,128)(2,1)S(1)}, u32[]{:S(2)}, u32[]{:S(2)}) async-start(bf16[8,128,384]{2,1,0:T(8,128)(2,1)} %get-tuple-element.46), calls=%async_computation.2 | async-start | bytes 1572864 | tf_op jit(solution)/shard_map/cond/branch_1_fun/all_to_all | solution.py:261
  85.1 0.6 copy-start.1
